TPU v7x, 256 devices: a whole 4x4x8 slice. The times are simulated.
256 devices in a mesh: sensor: 64 (over y, x, z_lo), tm: 4 (over z_hi, core).
Axes of the slice: x: 4, y: 4, z: 8 (z_hi: 2, z_lo: 4; z = z_hi * 4 + z_lo), core: 2. Of those that a mesh axis runs over, the one named last changes fastest.
Arguments:
- series: bfloat16 [12, 8192, 128], P('tm', 'sensor'), may hold values from -40 to 40
- conv_weight: bfloat16 [3, 128, 256], replicated, may hold values from -0.3125 to 0.3125
- qk_weight: bfloat16 [2, 128, 128], replicated, may hold values from -1 to 1
- value_weight: bfloat16 [128, 128], replicated, may hold values from -0.5 to 0.5
- out_weight: bfloat16 [128, 128], replicated, may hold values from -0.5 to 0.5
- norm_gain: float32 [128], replicated, may hold values from 0.25 to 1.75
Outputs:
- layer_out: bfloat16 [12, 8192, 128], P('tm', 'sensor')
All inputs are finite; a program needn't handle non-finite values.
Results may differ from a plain program's by a relative error of at most 0.012.
The roundings to bfloat16 on the way count: a program that leaves them out, or rounds other values in their place, can miss the bound.
Values may be sent and summed in bfloat16 or wider, within the bound.
No kernel may reach another device: no remote copies, remote signals or barrier semaphores. Data moves between devices by JAX's collectives and lax.ppermute only.
A program may use at most 64 MiB of HBM per device.

v0:
```python
import math

import jax
import jax.numpy as jnp
from jax import lax
from jax.sharding import PartitionSpec as P

HEADS = 8


def from_behind(block, axis, distance):
    devices = range(lax.axis_size(axis))
    route = [(i - distance, i) for i in devices if i - distance in devices]
    return lax.ppermute(block, axis, route)


def local(series, conv_weight, qk_weight, value_weight, out_weight, norm_gain):
    steps_dev, sens_dev, width = series.shape
    head_dim = width // HEADS
    scale = 1.0 / math.sqrt(head_dim)
    taps = conv_weight.shape[0]
    rows = steps_dev * sens_dev
    earlier = from_behind(series[steps_dev - (taps - 1) :], "tm", 1)
    padded = jnp.concatenate([earlier, series], axis=0)
    conv = jnp.zeros((rows, 2 * width), jnp.float32)
    for tap in range(taps):
        window = padded[taps - 1 - tap : taps - 1 - tap + steps_dev].reshape(rows, width)
        conv = conv + jnp.dot(window, conv_weight[tap], preferred_element_type=jnp.float32)
    flat = series.reshape(rows, width).astype(jnp.float32)
    hidden = (flat + conv[:, :width] * jax.nn.sigmoid(conv[:, width:])).astype(jnp.bfloat16)
    query = jnp.dot(hidden, qk_weight[0], preferred_element_type=jnp.float32).astype(jnp.bfloat16)
    query = query.reshape(steps_dev, sens_dev, HEADS, head_dim)

    def absorb_block(carry, keys, values):
        maxima, totals, summed = carry
        count = keys.shape[1]
        keys = keys.reshape(steps_dev, count, HEADS, head_dim)
        values = values.reshape(steps_dev, count, HEADS, head_dim)
        scores = (
            jnp.einsum("tshd,tkhd->thsk", query, keys, preferred_element_type=jnp.float32) * scale
        )
        new_max = jnp.maximum(maxima, jnp.max(scores, axis=-1))
        correct = jnp.exp(maxima - new_max)
        probs = jnp.exp(scores - new_max[..., None])
        totals = totals * correct + jnp.sum(probs, axis=-1)
        added = jnp.einsum(
            "thsk,tkhd->thsd",
            probs.astype(jnp.bfloat16),
            values,
            preferred_element_type=jnp.float32,
        )
        summed = summed * correct[..., None] + added
        return (new_max, totals, summed)

    start_state = (
        jnp.full((steps_dev, HEADS, sens_dev), -1e30, jnp.float32),
        jnp.zeros((steps_dev, HEADS, sens_dev), jnp.float32),
        jnp.zeros((steps_dev, HEADS, sens_dev, head_dim), jnp.float32),
    )
    source = hidden.reshape(steps_dev, sens_dev, width)
    count = source.shape[1]
    source_rows = source.reshape(steps_dev * count, width)
    keys = jnp.dot(source_rows, qk_weight[1], preferred_element_type=jnp.float32).astype(
        jnp.bfloat16
    )
    values = jnp.dot(source_rows, value_weight, preferred_element_type=jnp.float32).astype(
        jnp.bfloat16
    )
    own_keys = keys.reshape(steps_dev, count, width)
    own_values = values.reshape(steps_dev, count, width)
    keys = lax.all_gather(own_keys, "sensor", axis=1, tiled=True)
    count = keys.shape[1]
    block = math.gcd(count, 512)
    nblocks = count // block
    key_blocks = jnp.moveaxis(keys.reshape(steps_dev, nblocks, block, width), 1, 0)
    value_blocks = jnp.moveaxis(
        lax.all_gather(own_values, "sensor", axis=1, tiled=True).reshape(
            steps_dev, nblocks, block, width
        ),
        1,
        0,
    )

    def one_turn(state, pair):
        return (absorb_block(state, pair[0], pair[1]), None)

    final, unused = lax.scan(one_turn, start_state, (key_blocks, value_blocks))
    maxima, totals, summed = final
    attended = summed / totals[..., None]
    attended = jnp.transpose(attended, (0, 2, 1, 3)).reshape(rows, width).astype(jnp.bfloat16)
    mixed = jnp.dot(attended, out_weight, preferred_element_type=jnp.float32) + hidden.astype(
        jnp.float32
    )
    mean = jnp.mean(mixed, axis=-1, keepdims=True)
    var = jnp.mean((mixed - mean) ** 2, axis=-1, keepdims=True)
    normed = (mixed - mean) / jnp.sqrt(var + 1e-05) * norm_gain
    return normed.reshape(steps_dev, sens_dev, width).astype(jnp.bfloat16)


def solution(mesh):
    in_specs = (P("tm", "sensor", None), P(), P(), P(), P(), P())
    out_specs = P("tm", "sensor", None)
    return jax.shard_map(local, mesh=mesh, in_specs=in_specs, out_specs=out_specs, check_vma=False)
```

profile of v0, /device:TPU:192, one launch (start us, length us, event | category | flops | bytes accessed | tf_op | source)
XLA Modules:
  0.0 843.7 jit_solution(4332230592460186080)
XLA Ops:
  7.4 1.9 collective-permute-start
  10.4 6.5 collective-permute-done
  20.9 1.6 convolution_convert_fusion
  22.5 1.6 convolution_convert_fusion.2
  25.2 364.8 %all-gather.5.cloned.1.call-done = bf16[3,8192,128]{2,1,0:T(8,128)(2,1)} async-done(((bf16[3,128,128]{2,1,0:T(8,128)(2,1)}), bf16[3,8192,128]{2,1,0:T(8,128)(2,1)}) %all-gather.5.cloned.1.call-update) | async-done | bytes 6291472 | tf_op jit(solution)/shard_map/all_gather | solution.py:77
  390.0 368.4 %all-gather.3.cloned.1.call-done = bf16[3,8192,128]{2,1,0:T(8,128)(2,1)} async-done(((bf16[3,128,128]{2,1,0:T(8,128)(2,1)}), bf16[3,8192,128]{2,1,0:T(8,128)(2,1)}) %all-gather.3.cloned.1.call-update) | async-done | bytes 6291472 | tf_op jit(solution)/shard_map/all_gather | solution.py:71
  758.5 76.8 %while.15 = (s32[]{:T(128)}, f32[3,8,128]{2,1,0:T(8,128)S(1)}, f32[3,8,128]{2,1,0:T(8,128)S(1)}, f32[3,8,128,16]{2,3,1,0:T(8,128)S(1)}, bf16[16,3,512,128]{3,2,0...) while((s32[]{:T(128)}, f32[3,8,128]{2,1,0:T(8,128)S(1)}, ...), condition=%wide.region_3.4_spmd.clone, body=%wide.region_0.3_spmd.clone.sunk | while | flops 113409024 | bytes 23494772 | solution.py:87
  758.5 1.2 constant_dynamic-slice_fusion.3
  760.0 1.1 bitcast_reduce_fusion.2
  763.3 1.2 constant_dynamic-slice_fusion.3
  768.1 1.2 constant_dynamic-slice_fusion.3
  772.9 1.2 constant_dynamic-slice_fusion.3
  777.7 1.2 constant_dynamic-slice_fusion.3
  779.2 1.1 bitcast_reduce_fusion.2
  782.5 1.2 constant_dynamic-slice_fusion.3
  784.1 1.1 bitcast_reduce_fusion.2
  787.3 1.2 constant_dynamic-slice_fusion.3
  788.9 1.1 bitcast_reduce_fusion.2
  792.1 1.2 constant_dynamic-slice_fusion.3
  796.9 1.2 constant_dynamic-slice_fusion.3
  798.5 1.1 bitcast_reduce_fusion.2
  801.7 1.2 constant_dynamic-slice_fusion.3
  803.3 1.1 bitcast_reduce_fusion.2
  806.5 1.2 constant_dynamic-slice_fusion.3
  811.3 1.2 constant_dynamic-slice_fusion.3
  816.1 1.2 constant_dynamic-slice_fusion.3
  820.9 1.2 constant_dynamic-slice_fusion.3
  822.5 1.1 bitcast_reduce_fusion.2
  825.7 1.2 constant_dynamic-slice_fusion.3
  827.3 1.1 bitcast_reduce_fusion.2
  830.5 1.2 constant_dynamic-slice_fusion.3
  832.1 1.1 bitcast_reduce_fusion.2
  (149 shorter events, 56.3 us)
Async XLA Ops:
  6.5 828.9 %copy-start = (bf16[128,128]{1,0:T(8,128)(2,1)S(1)}, bf16[128,128]{1,0:T(8,128)(2,1)}, u32[]{:S(2)}) copy-start(bf16[128,128]{1,0:T(8,128)(2,1)} %param.12) | copy-start | bytes 98308
  6.5 383.5 %all-gather.5.cloned.1.call-start = ((), (), s32[]{:S(2)}) async-start(), calls=%async_computation.1 | async-start | bytes 6389760 | tf_op jit(solution)/shard_map/all_gather | solution.py:77
  7.4 9.5 %collective-permute-start = (bf16[2,128,128]{2,1,0:T(8,128)(2,1)S(1)}, bf16[2,128,128]{2,1,0:T(8,128)(2,1)S(1)}, u32[]{:S(2)}, u32[]{:S(2)}) collective-permute-start(bf16[2,128,128]{2,1,0:T(8,128)(2,1)S(1)} %slice.31), channel_id=1, source_target_pairs={{0,1},{1,2},{2,3},{4,5},{5,6},{6,7},{8,9},{9,10},{10,11},{12,13},{... | collective-permute-start | bytes 196616 | tf_op jit(solution)/shard_map/ppermute | solution.py:14
  22.5 736.0 %all-gather.3.cloned.1.call-start = ((), (), s32[]{:S(2)}) async-start(), calls=%async_computation | async-start | bytes 6389760 | tf_op jit(solution)/shard_map/all_gather | solution.py:71
  758.5 77.6 %copy-start.1 = (f32[128]{0:T(128)S(1)}, f32[128]{0:T(128)}, u32[]{:S(2)}) copy-start(f32[128]{0:T(128)} %param.13) | copy-start | bytes 1540
Sparse Core Ops, SparseCore 0:
  22.6 367.4 all-gather.4
  391.8 366.6 all-gather.2
where the time goes:
time: 848 us; the launch traced here: 844 us
  waiting for transfers between devices  740 us (87%)
  matrix products  41.9 us (5%)
  local copies, waits for them, and re-layouts  26.8 us (3%)
  other arithmetic  19.1 us (2%)
  between operations  13.5 us (2%)
    all_gather x1, waiting for transfers between devices, local(): keys = lax.all_gather(own_keys, 'sensor', axis=1, tiled=True)  368 us
    all_gather x1, waiting for transfers between devices, local(): lax.all_gather(own_values, 'sensor', axis=1, tiled=True)  365 us
    dynamic_slice x48, local copies, waits for them, and re-layouts, local(): final, unused = lax.scan(one_turn, start_state, (key_blocks, value_blocks))  24.7 us
    dot_general x16, matrix products, absorb_block(): jnp.einsum('tshd,tkhd->thsk', query, keys, preferred_element_type=jnp.flo...  17.3 us
    dot_general x16, matrix products, absorb_block(): jnp.einsum('thsk,tkhd->thsd', probs.astype(jnp.bfloat16), values, preferr...  17.1 us
  transfers between devices with their start and end apart: 3, of which 3 were waited for; matrix products, arithmetic and copies ran while one was open for 0% of the time, Pallas kernels for 0%

commit v1 on v0

v1 whole, which is shorter than its diff:
```python
import functools

import jax
import jax.numpy as jnp
from jax import lax
from jax.experimental import pallas as pl
from jax.experimental.pallas import tpu as pltpu
from jax.sharding import Mesh, PartitionSpec as P

F32 = jnp.float32
BF16 = jnp.bfloat16
HEADS = 8
HEAD_DIM = 16
LOG2E = 1.4426950408889634
AXES = ("y1", "y0", "x1", "x0", "z1", "z0", "zh", "core")
SENSOR = AXES[:6]
TM = AXES[6:]
NEAR = ("y0", "x0", "z0")
FAR = ("y1", "x1", "z1")
VMEM = pl.BlockSpec(memory_space=pltpu.VMEM)
KEYS = 2048
LOWEST = 2.0**-20
HIGHEST = 2.0**100


def split3(x):
    high = x.astype(BF16)
    rest = x - high.astype(F32)
    mid = rest.astype(BF16)
    low = (rest - mid.astype(F32)).astype(BF16)
    return high, mid, low


def first_kernel(earlier, series, conv_w, qk_w, value_w, hidden_ref, qkv_ref):
    steps, sens, width = series.shape
    own = series[...].reshape(steps * sens, width)
    padded = jnp.concatenate([earlier[...].reshape(2 * sens, width), own], axis=0)
    conv = jnp.dot(own, conv_w[0], preferred_element_type=F32)
    for tap in (1, 2):
        window = padded[(2 - tap) * sens : (2 - tap + steps) * sens]
        conv = conv + jnp.dot(window, conv_w[tap], preferred_element_type=F32)
    gate = jax.nn.sigmoid(conv[:, width:])
    hidden = (own.astype(F32) + conv[:, :width] * gate).astype(BF16)
    hidden_ref[...] = hidden
    for part, weight in enumerate((qk_w[0], qk_w[1], value_w[...])):
        rows = jnp.dot(hidden, weight, preferred_element_type=F32).astype(BF16)
        for t in range(steps):
            cols = rows[t * sens : (t + 1) * sens].T
            for h in range(HEADS):
                qkv_ref[h, t, part * HEAD_DIM : (part + 1) * HEAD_DIM, :] = cols[
                    h * HEAD_DIM : (h + 1) * HEAD_DIM
                ]


def attention_kernel(qkv, *refs):
    chunks, out_ref, ka, qa, va, qs = refs[:-5], refs[-5], refs[-4], refs[-3], refs[-2], refs[-1]
    blocks, steps, _, lanes = qkv.shape
    nq = blocks * lanes
    nk = len(chunks) * blocks * lanes
    pairs = blocks // 2
    one = jnp.ones((16, 2 * lanes), BF16)

    def prepare(t):
        for c, chunk in enumerate(chunks):
            for p in range(pairs):
                kv = jnp.concatenate([chunk[2 * p, t], chunk[2 * p + 1, t]], axis=1)
                k = kv[:HEAD_DIM]
                row = (c * pairs + p) * 2 * lanes
                ka[row : row + 2 * lanes, :] = jnp.concatenate([k, k, k, one], axis=0).T
                va[c * pairs + p] = jnp.concatenate([kv[HEAD_DIM:], one], axis=0)
        for b in range(blocks):
            q = qkv[b, t, :HEAD_DIM, :]
            qs[:, b * lanes : (b + 1) * lanes] = q
            parts = split3(q.astype(F32) * (0.25 * LOG2E))
            qa[:48, b * lanes : (b + 1) * lanes] = jnp.concatenate(parts, axis=0)

    def store(t, value):
        for b in range(blocks):
            out_ref[b, t] = value[:, b * lanes : (b + 1) * lanes].astype(BF16)

    def fast(t, bad):
        prepare(t)
        sample = jnp.dot(ka[:256, :48], qa[:48, :], preferred_element_type=F32)
        shift = split3(-jnp.max(sample, axis=0, keepdims=True))
        row = lax.broadcasted_iota(jnp.int32, (16, nq), 0)
        rows = jnp.zeros((16, nq), F32)
        for i, part in enumerate(shift):
            rows = jnp.where(row == i, part.astype(F32), rows)
        qa[48:, :] = rows.astype(BF16)
        qq = qa[...]

        def block(i, acc):
            off = pl.multiple_of(i * KEYS, KEYS)
            s = jnp.dot(ka[pl.ds(off, KEYS), :], qq, preferred_element_type=F32)
            p = jnp.exp2(s).astype(BF16)
            for u in range(KEYS // 256):
                acc = acc + jnp.dot(
                    va[i * (KEYS // 256) + u],
                    p[u * 256 : (u + 1) * 256],
                    preferred_element_type=F32,
                )
            return acc

        acc = lax.fori_loop(0, nk // KEYS, block, jnp.zeros((32, nq), F32))
        total = acc[HEAD_DIM : HEAD_DIM + 1]
        store(t, acc[:HEAD_DIM] / total)
        good = (total >= LOWEST) & (total <= HIGHEST)
        return jnp.maximum(bad, jnp.where(good, 0.0, 1.0))

    bad = lax.fori_loop(0, steps, fast, jnp.zeros((1, nq), F32))

    @pl.when(jnp.max(bad) > 0.0)
    def exact():
        def step(t, carry):
            prepare(t)
            qq = qs[...]

            def scores(i):
                off = pl.multiple_of(i * 256, 256)
                k = ka[pl.ds(off, 256), :HEAD_DIM]
                return jnp.dot(k, qq, preferred_element_type=F32) * 0.25

            def largest(i, top):
                return jnp.maximum(top, jnp.max(scores(i), axis=0, keepdims=True))

            top = lax.fori_loop(0, nk // 256, largest, jnp.full((1, nq), -jnp.inf, F32))

            def block(i, acc):
                p = jnp.exp(scores(i) - top).astype(BF16)
                return acc + jnp.dot(va[i], p, preferred_element_type=F32)

            acc = lax.fori_loop(0, nk // 256, block, jnp.zeros((32, nq), F32))
            store(t, acc[:HEAD_DIM] / acc[HEAD_DIM : HEAD_DIM + 1])
            return carry

        lax.fori_loop(0, steps, step, 0)


def last_kernel(attended, hidden, out_w, gain, out_ref):
    heads, steps, dim, sens = attended.shape
    width = heads * dim
    for t in range(steps):
        rows = attended[:, t].reshape(width, sens).T
        mixed = jnp.dot(rows, out_w[...], preferred_element_type=F32)
        mixed = mixed + hidden[t * sens : (t + 1) * sens, :].astype(F32)
        mean = jnp.mean(mixed, axis=-1, keepdims=True)
        centred = mixed - mean
        var = jnp.mean(centred * centred, axis=-1, keepdims=True)
        out_ref[t] = (centred / jnp.sqrt(var + 1e-5) * gain[...]).astype(BF16)


def local(series, conv_weight, qk_weight, value_weight, out_weight, norm_gain):
    steps, sens, width = series.shape
    blocks = lax.axis_size(TM)
    earlier = lax.ppermute(series[steps - 2 :], TM, [(i, i + 1) for i in range(blocks - 1)])
    hidden, qkv = pl.pallas_call(
        first_kernel,
        out_shape=(
            jax.ShapeDtypeStruct((steps * sens, width), BF16),
            jax.ShapeDtypeStruct((HEADS, steps, 3 * HEAD_DIM, sens), BF16),
        ),
        in_specs=[VMEM] * 5,
        out_specs=(VMEM, VMEM),
        compiler_params=pltpu.CompilerParams(vmem_limit_bytes=32 << 20),
    )(earlier, series, conv_weight, qk_weight, value_weight)
    qkv = lax.all_to_all(qkv, NEAR, 0, 0, tiled=True)
    kv = qkv[:, :, HEAD_DIM:, :]
    groups = lax.axis_size(FAR)
    chunks = [kv]
    for mask in range(1, groups):
        chunks.append(lax.ppermute(kv, FAR, [(i, i ^ mask) for i in range(groups)]))
    near = qkv.shape[0]
    nq, nk = near * sens, groups * near * sens
    attended = pl.pallas_call(
        attention_kernel,
        out_shape=jax.ShapeDtypeStruct((near, steps, HEAD_DIM, sens), BF16),
        in_specs=[VMEM] * (1 + groups),
        out_specs=VMEM,
        scratch_shapes=[
            pltpu.VMEM((nk, 64), BF16),
            pltpu.VMEM((64, nq), BF16),
            pltpu.VMEM((nk // 256, 32, 256), BF16),
            pltpu.VMEM((HEAD_DIM, nq), BF16),
        ],
        compiler_params=pltpu.CompilerParams(vmem_limit_bytes=48 << 20),
    )(qkv, *chunks)
    attended = lax.all_to_all(attended, NEAR, 0, 0, tiled=True)
    return pl.pallas_call(
        last_kernel,
        out_shape=jax.ShapeDtypeStruct((steps, sens, width), BF16),
        in_specs=[VMEM] * 4,
        out_specs=VMEM,
        compiler_params=pltpu.CompilerParams(vmem_limit_bytes=32 << 20),
    )(attended, hidden, out_weight, norm_gain.reshape(1, width))


def solution(mesh):
    fine = Mesh(mesh.devices.reshape((2,) * len(AXES)), AXES)
    spec = P(TM, SENSOR, None)
    return jax.shard_map(
        local,
        mesh=fine,
        in_specs=(spec, P(), P(), P(), P(), P()),
        out_specs=spec,
        check_vma=False,
    )
```

time: 848 us -> 165 us (0.19)
  waiting for transfers between devices: 740 us -> 16.7 us
  Pallas kernels: 0 us -> 95.5 us
  matrix products: 41.9 us -> 0 us
  blocking collectives: 0 us -> 26.4 us
  local copies, waits for them, and re-layouts: 26.8 us -> 3.36 us
  starting transfers between devices: 1.95 us -> 21.1 us
  other arithmetic: 19.1 us -> 0 us
  between operations: 13.5 us -> 0.05 us
    all_gather x2 -> x0, waiting for transfers between devices: 733 us -> none  [the longest x1 368 us: local(): keys = lax.all_gather(own_keys, 'sensor', axis=1, tiled=True)]
    pallas_call x0 -> x3, Pallas kernels: none -> 95.5 us  [the longest x1 93.8 us: local(): pl.pallas_call(attention_kernel, out_shape=jax.ShapeDtypeStruct((near, st...]
    dot_general x39 -> x0, matrix products: 41.9 us -> none  [the longest x16 17.3 us: absorb_block(): jnp.einsum('tshd,tkhd->thsk', query, keys, preferred_element_type=jnp.flo...]
    all_to_all x0 -> x2, blocking collectives: none -> 26.4 us  [the longest x1 13.3 us: local(): attended = lax.all_to_all(attended, NEAR, 0, 0, tiled=True)]
    dynamic_slice x48 -> x0, local copies, waits for them, and re-layouts: 24.7 us -> none  [local(): final, unused = lax.scan(one_turn, start_state, (key_blocks, value_blocks))]
    ppermute x1 -> x8, starting transfers between devices: 1.91 us -> 21.1 us  [the longest x7 19.2 us: local(): chunks.append(lax.ppermute(kv, FAR, [(i, i ^ mask) for i in range(groups)]))]
    reduce_sum x17 -> x0, other arithmetic: 16.9 us -> none  [the longest x16 16.7 us: absorb_block(): totals = totals * correct + jnp.sum(probs, axis=-1)]
    ppermute x1 -> x8, waiting for transfers between devices: 6.48 us -> 16.7 us  [the longest x7 9.09 us: local(): chunks.append(lax.ppermute(kv, FAR, [(i, i ^ mask) for i in range(groups)]))]
  transfers between devices with their start and end apart: 3 -> 8, of which waited for: 3 -> 5; matrix products, arithmetic and copies ran while one was open for 0% -> 0% of each run, Pallas kernels for 0% -> 0%
where the time goes in v1:
time: 165 us; the launch traced here: 163 us
  Pallas kernels  95.5 us (58%)
  blocking collectives  26.4 us (16%)
  starting transfers between devices  21.1 us (13%)
  waiting for transfers between devices  16.7 us (10%)
  local copies, waits for them, and re-layouts  3.36 us (2%)
    pallas_call x1, Pallas kernels, local(): pl.pallas_call(attention_kernel, out_shape=jax.ShapeDtypeStruct((near, st...  93.8 us
    ppermute x7, starting transfers between devices, local(): chunks.append(lax.ppermute(kv, FAR, [(i, i ^ mask) for i in range(groups)]))  19.2 us
    all_to_all x1, blocking collectives, local(): attended = lax.all_to_all(attended, NEAR, 0, 0, tiled=True)  13.3 us
    all_to_all x1, blocking collectives, local(): qkv = lax.all_to_all(qkv, NEAR, 0, 0, tiled=True)  13.1 us
    ppermute x7, waiting for transfers between devices, local(): chunks.append(lax.ppermute(kv, FAR, [(i, i ^ mask) for i in range(groups)]))  9.09 us
    ppermute x1, waiting for transfers between devices, local(): lax.ppermute(series[steps - 2:], TM, [(i, i + 1) for i in range(blocks -...  7.56 us
  transfers between devices with their start and end apart: 8, of which 5 were waited for; matrix products, arithmetic and copies ran while one was open for 0% of the time, Pallas kernels for 0%

profile of v1, /device:TPU:192, one launch (start us, length us, event | category | flops | bytes accessed | tf_op | source)
XLA Modules:
  0.0 163.1 jit_solution(628837265126431076)
XLA Ops:
  0.0 0.0 copy-start
  0.0 0.9 slice.6
  0.9 1.9 %collective-permute-start = (bf16[2,128,128]{2,1,0:T(8,128)(2,1)S(1)}, bf16[2,128,128]{2,1,0:T(8,128)(2,1)S(1)}, u32[]{:S(2)}, u32[]{:S(2)}) collective-permute-start(bf16[2,128,128]{2,1,0:T(8,128)(2,1)S(1)} %slice.6), channel_id=1, source_target_pairs={{0,1},{1,2},{2,3},{4,5},{5,6},{6,7},{8,9},{9,10},{10,11},{12,13},{... | collective-permute-start | bytes 196616 | tf_op jit(solution)/shard_map/ppermute | solution.py:155
  2.8 7.6 %collective-permute-done.earlier = bf16[2,128,128]{2,1,0:T(8,128)(2,1)S(1)} collective-permute-done((bf16[2,128,128]{2,1,0:T(8,128)(2,1)S(1)}, bf16[2,128,128]{2,1,0:T(8,128)(2,1)S(1)}, u32[]{:S(2)}, u32[]{:S(2)}) %collective-permute-start) | collective-permute-done | bytes 65568 | tf_op jit(solution)/shard_map/ppermute | solution.py:155
  10.4 0.0 copy-done
  10.4 0.0 copy-done.3
  10.4 0.0 copy-start.1
  10.4 0.9 copy-done.1
  11.3 0.0 copy-start.2
  11.3 0.8 copy-done.2
  12.2 0.7 shard_map.64
  12.8 13.1 %all_to_all.10.qkv = bf16[8,3,48,128]{3,2,1,0:T(8,128)(2,1)S(1)} all-to-all(bf16[8,3,48,128]{3,2,1,0:T(8,128)(2,1)S(1)} %get-tuple-element.7), channel_id=1, replica_groups=mesh['y1'=2,'y0'=2,'x1'=2,'x0'=2,'z1'=2,'z0'=2,'zh'=2,'core'=2] {'y0','x..., dimensions={0} | all-to-all | bytes 589824 | tf_op jit(solution)/shard_map/all_to_all | solution.py:166
  26.0 6.3 %collective-permute-start.7 = (bf16[8,3,32,128]{3,2,1,0:T(8,128)(2,1)S(1)}, bf16[8,3,32,128]{3,2,1,0:T(8,128)(2,1)S(1)}, u32[]{:S(2)}, u32[]{:S(2)}) collective-permute-start(bf16[8,3,32,128]{3,2,1,0:T(8,128)(2,1)S(1)} %slice.8.refs_0_), channel_id=1, source_target_pairs={{0,168},{8,160},{32,136},{40,128},{128,40},{136,32},{160,8},{168,0... | collective-permute-start | bytes 589832 | tf_op jit(solution)/shard_map/ppermute | solution.py:171
  32.3 0.0 collective-permute-start.6
  32.3 3.6 %collective-permute-start.5 = (bf16[8,3,32,128]{3,2,1,0:T(8,128)(2,1)S(1)}, bf16[8,3,32,128]{3,2,1,0:T(8,128)(2,1)S(1)}, u32[]{:S(2)}, u32[]{:S(2)}) collective-permute-start(bf16[8,3,32,128]{3,2,1,0:T(8,128)(2,1)S(1)} %slice.8.refs_0_), channel_id=1, source_target_pairs={{0,136},{8,128},{32,168},{40,160},{128,8},{136,0},{160,40},{168,32... | collective-permute-start | bytes 589832 | tf_op jit(solution)/shard_map/ppermute | solution.py:171
  35.9 1.4 collective-permute-start.4
  37.3 3.3 %collective-permute-start.3 = (bf16[8,3,32,128]{3,2,1,0:T(8,128)(2,1)S(1)}, bf16[8,3,32,128]{3,2,1,0:T(8,128)(2,1)S(1)}, u32[]{:S(2)}, u32[]{:S(2)}) collective-permute-start(bf16[8,3,32,128]{3,2,1,0:T(8,128)(2,1)S(1)} %slice.8.refs_0_), channel_id=1, source_target_pairs={{0,40},{8,32},{32,8},{40,0},{128,168},{136,160},{160,136},{168,128... | collective-permute-start | bytes 589832 | tf_op jit(solution)/shard_map/ppermute | solution.py:171
  40.6 5.3 %collective-permute-done.7.refs_7_ = bf16[8,3,32,128]{3,2,1,0:T(8,128)(2,1)S(1)} collective-permute-done((bf16[8,3,32,128]{3,2,1,0:T(8,128)(2,1)S(1)}, bf16[8,3,32,128]{3,2,1,0:T(8,128)(2,1)S(1)}, u32[]{:S(2)}, u32[]{:S(2)}) %collective-permute-start.7) | collective-permute-done | bytes 196640 | tf_op jit(solution)/shard_map/ppermute | solution.py:171
  45.9 0.3 collective-permute-start.2
  46.2 0.0 collective-permute-done.6.refs_6_
  46.2 4.3 %collective-permute-start.1 = (bf16[8,3,32,128]{3,2,1,0:T(8,128)(2,1)S(1)}, bf16[8,3,32,128]{3,2,1,0:T(8,128)(2,1)S(1)}, u32[]{:S(2)}, u32[]{:S(2)}) collective-permute-start(bf16[8,3,32,128]{3,2,1,0:T(8,128)(2,1)S(1)} %slice.8.refs_0_), channel_id=1, source_target_pairs={{0,8},{8,0},{32,40},{40,32},{128,136},{136,128},{160,168},{168,160... | collective-permute-start | bytes 589832 | tf_op jit(solution)/shard_map/ppermute | solution.py:171
  50.5 0.0 collective-permute-done.5.refs_5_
  50.5 0.0 collective-permute-done.4.refs_4_
  50.5 1.4 collective-permute-done.3.refs_3_
  51.9 1.2 collective-permute-done.2.refs_2_
  53.1 1.1 collective-permute-done.1.refs_1_
  54.3 93.8 %shard_map.65 = bf16[8,3,16,128]{3,2,1,0:T(8,128)(2,1)S(1)} custom-call(bf16[8,3,48,128]{3,2,1,0:T(8,128)(2,1)S(1)} %all_to_all.10.qkv, bf16[8,3,32,128]{3,2,1,0:T(8,128)(2,1)S(1)} %slice.8.refs_0_, bf16[8,3,32,128]{3,2,1,0:T(8,128)(2,1)S(1)} %collective-permute-done.1.refs_1_, bf16[8,3,32,128]{3,2,1,0:T(8,128)(2,1)S(1)} %collective-permute-done.2.refs_2_, ...), custom_call_target="tpu_custom_call" | custom-call | tf_op jit(solution)/shard_map/pallas_call | solution.py:174
  148.1 0.0 copy-start.4
  148.1 13.3 %all_to_all.11.attended = bf16[8,3,16,128]{3,2,1,0:T(8,128)(2,1)S(1)} all-to-all(bf16[8,3,16,128]{3,2,1,0:T(8,128)(2,1)S(1)} %shard_map.65), channel_id=1, replica_groups=mesh['y1'=2,'y0'=2,'x1'=2,'x0'=2,'z1'=2,'z0'=2,'zh'=2,'core'=2] {'y0','x..., dimensions={0} | all-to-all | bytes 196608 | tf_op jit(solution)/shard_map/all_to_all | solution.py:187
  161.4 0.0 copy-done.4
  161.4 0.7 copy-done.5
  162.1 1.1 shard_map.66
  (3 shorter events, 0.0 us)
Async XLA Ops:
  0.0 10.4 %copy-start = (bf16[3,128,128]{2,1,0:T(8,128)(2,1)S(1)}, bf16[3,128,128]{2,1,0:T(8,128)(2,1)}, u32[]{:S(2)}) copy-start(bf16[3,128,128]{2,1,0:T(8,128)(2,1)} %series.1) | copy-start | bytes 294916
  0.0 10.4 %copy-start.3 = (bf16[128,128]{1,0:T(8,128)(2,1)S(1)}, bf16[128,128]{1,0:T(8,128)(2,1)}, u32[]{:S(2)}) copy-start(bf16[128,128]{1,0:T(8,128)(2,1)} %value_w.1) | copy-start | bytes 98308
  0.9 9.5 %collective-permute-start = (bf16[2,128,128]{2,1,0:T(8,128)(2,1)S(1)}, bf16[2,128,128]{2,1,0:T(8,128)(2,1)S(1)}, u32[]{:S(2)}, u32[]{:S(2)}) collective-permute-start(bf16[2,128,128]{2,1,0:T(8,128)(2,1)S(1)} %slice.6), channel_id=1, source_target_pairs={{0,1},{1,2},{2,3},{4,5},{5,6},{6,7},{8,9},{9,10},{10,11},{12,13},{... | collective-permute-start | bytes 196616 | tf_op jit(solution)/shard_map/ppermute | solution.py:155
  10.4 0.9 copy-start.1
  11.3 0.8 copy-start.2
  26.0 20.0 %collective-permute-start.7 = (bf16[8,3,32,128]{3,2,1,0:T(8,128)(2,1)S(1)}, bf16[8,3,32,128]{3,2,1,0:T(8,128)(2,1)S(1)}, u32[]{:S(2)}, u32[]{:S(2)}) collective-permute-start(bf16[8,3,32,128]{3,2,1,0:T(8,128)(2,1)S(1)} %slice.8.refs_0_), channel_id=1, source_target_pairs={{0,168},{8,160},{32,136},{40,128},{128,40},{136,32},{160,8},{168,0... | collective-permute-start | bytes 589832 | tf_op jit(solution)/shard_map/ppermute | solution.py:171
  32.3 13.9 %collective-permute-start.6 = (bf16[8,3,32,128]{3,2,1,0:T(8,128)(2,1)S(1)}, bf16[8,3,32,128]{3,2,1,0:T(8,128)(2,1)S(1)}, u32[]{:S(2)}, u32[]{:S(2)}) collective-permute-start(bf16[8,3,32,128]{3,2,1,0:T(8,128)(2,1)S(1)} %slice.8.refs_0_), channel_id=1, source_target_pairs={{0,160},{8,168},{32,128},{40,136},{128,32},{136,40},{160,0},{168,8... | collective-permute-start | bytes 589832 | tf_op jit(solution)/shard_map/ppermute | solution.py:171
  32.3 18.2 %collective-permute-start.5 = (bf16[8,3,32,128]{3,2,1,0:T(8,128)(2,1)S(1)}, bf16[8,3,32,128]{3,2,1,0:T(8,128)(2,1)S(1)}, u32[]{:S(2)}, u32[]{:S(2)}) collective-permute-start(bf16[8,3,32,128]{3,2,1,0:T(8,128)(2,1)S(1)} %slice.8.refs_0_), channel_id=1, source_target_pairs={{0,136},{8,128},{32,168},{40,160},{128,8},{136,0},{160,40},{168,32... | collective-permute-start | bytes 589832 | tf_op jit(solution)/shard_map/ppermute | solution.py:171
  35.9 14.6 %collective-permute-start.4 = (bf16[8,3,32,128]{3,2,1,0:T(8,128)(2,1)S(1)}, bf16[8,3,32,128]{3,2,1,0:T(8,128)(2,1)S(1)}, u32[]{:S(2)}, u32[]{:S(2)}) collective-permute-start(bf16[8,3,32,128]{3,2,1,0:T(8,128)(2,1)S(1)} %slice.8.refs_0_), channel_id=1, source_target_pairs={{0,128},{8,136},{32,160},{40,168},{128,0},{136,8},{160,32},{168,40... | collective-permute-start | bytes 589832 | tf_op jit(solution)/shard_map/ppermute | solution.py:171
  37.3 14.6 %collective-permute-start.3 = (bf16[8,3,32,128]{3,2,1,0:T(8,128)(2,1)S(1)}, bf16[8,3,32,128]{3,2,1,0:T(8,128)(2,1)S(1)}, u32[]{:S(2)}, u32[]{:S(2)}) collective-permute-start(bf16[8,3,32,128]{3,2,1,0:T(8,128)(2,1)S(1)} %slice.8.refs_0_), channel_id=1, source_target_pairs={{0,40},{8,32},{32,8},{40,0},{128,168},{136,160},{160,136},{168,128... | collective-permute-start | bytes 589832 | tf_op jit(solution)/shard_map/ppermute | solution.py:171
  45.9 7.2 %collective-permute-start.2 = (bf16[8,3,32,128]{3,2,1,0:T(8,128)(2,1)S(1)}, bf16[8,3,32,128]{3,2,1,0:T(8,128)(2,1)S(1)}, u32[]{:S(2)}, u32[]{:S(2)}) collective-permute-start(bf16[8,3,32,128]{3,2,1,0:T(8,128)(2,1)S(1)} %slice.8.refs_0_), channel_id=1, source_target_pairs={{0,32},{8,40},{32,0},{40,8},{128,160},{136,168},{160,128},{168,136... | collective-permute-start | bytes 589832 | tf_op jit(solution)/shard_map/ppermute | solution.py:171
  46.2 8.0 %collective-permute-start.1 = (bf16[8,3,32,128]{3,2,1,0:T(8,128)(2,1)S(1)}, bf16[8,3,32,128]{3,2,1,0:T(8,128)(2,1)S(1)}, u32[]{:S(2)}, u32[]{:S(2)}) collective-permute-start(bf16[8,3,32,128]{3,2,1,0:T(8,128)(2,1)S(1)} %slice.8.refs_0_), channel_id=1, source_target_pairs={{0,8},{8,0},{32,40},{40,32},{128,136},{136,128},{160,168},{168,160... | collective-permute-start | bytes 589832 | tf_op jit(solution)/shard_map/ppermute | solution.py:171
  148.1 13.3 %copy-start.4 = (bf16[128,128]{1,0:T(8,128)(2,1)S(1)}, bf16[128,128]{1,0:T(8,128)(2,1)}, u32[]{:S(2)}) copy-start(bf16[128,128]{1,0:T(8,128)(2,1)} %out_w.1) | copy-start | bytes 98308
  161.4 0.7 copy-start.5

commit v2 on v1

v2 whole, which is shorter than its diff:
```python
import functools

import jax
import jax.numpy as jnp
from jax import lax
from jax.experimental import pallas as pl
from jax.experimental.pallas import tpu as pltpu
from jax.sharding import Mesh, PartitionSpec as P

F32 = jnp.float32
BF16 = jnp.bfloat16
HEADS = 8
HEAD_DIM = 16
LOG2E = 1.4426950408889634
AXES = ("y1", "y0", "x1", "x0", "z1", "z0", "zh", "core")
SENSOR = AXES[:6]
TM = AXES[6:]
NEAR = ("y0", "x0", "z0")
VMEM = pl.BlockSpec(memory_space=pltpu.VMEM)
SMEM = pl.BlockSpec(memory_space=pltpu.SMEM)
LOWEST = 2.0**-20
HIGHEST = 2.0**100


def split3(x):
    high = x.astype(BF16)
    rest = x - high.astype(F32)
    mid = rest.astype(BF16)
    low = (rest - mid.astype(F32)).astype(BF16)
    return high, mid, low


def first_kernel(mirror, earlier, series, conv_w, qk_w, value_w, hidden_ref, qkv_ref):
    flip = mirror[0]
    steps, sens, width = series.shape
    own = series[...].reshape(steps * sens, width)
    padded = jnp.concatenate([earlier[...].reshape(2 * sens, width), own], axis=0)
    conv = jnp.dot(own, conv_w[0], preferred_element_type=F32)
    for tap in (1, 2):
        window = padded[(2 - tap) * sens : (2 - tap + steps) * sens]
        conv = conv + jnp.dot(window, conv_w[tap], preferred_element_type=F32)
    gate = jax.nn.sigmoid(conv[:, width:])
    hidden = (own.astype(F32) + conv[:, :width] * gate).astype(BF16)
    hidden_ref[...] = hidden
    for part, weight in enumerate((qk_w[0], qk_w[1], value_w[...])):
        rows = jnp.dot(hidden, weight, preferred_element_type=F32).astype(BF16)
        for t in range(steps):
            cols = rows[t * sens : (t + 1) * sens].T
            for h in range(HEADS):
                qkv_ref[h ^ flip, t, part * HEAD_DIM : (part + 1) * HEAD_DIM, :] = cols[
                    h * HEAD_DIM : (h + 1) * HEAD_DIM
                ]


def absorb(t, qq, acc, chunks, ka, va):
    blocks, lanes = chunks[0].shape[0], chunks[0].shape[3]
    one = jnp.ones((16, 2 * lanes), BF16)
    for c, chunk in enumerate(chunks):
        for p in range(blocks // 2):
            kv = jnp.concatenate([chunk[2 * p, t, -32:], chunk[2 * p + 1, t, -32:]], axis=1)
            k = kv[:HEAD_DIM]
            pair = c * (blocks // 2) + p
            ka[pair * 256 : (pair + 1) * 256, :] = jnp.concatenate([k, k, k, one], axis=0).T
            va[pair] = jnp.concatenate([kv[HEAD_DIM:], one], axis=0)
    pairs = len(chunks) * (blocks // 2)
    s = jnp.dot(ka[: pairs * 256, :], qq, preferred_element_type=F32)
    p = jnp.exp2(s).astype(BF16)
    for u in range(pairs):
        acc = acc + jnp.dot(va[u], p[u * 256 : (u + 1) * 256], preferred_element_type=F32)
    return acc


def begin_kernel(qkv, qa_ref, acc_ref, ka, va):
    blocks, steps, _, lanes = qkv.shape
    nq = blocks * lanes

    def step(t, carry):
        qa = qa_ref.at[t]
        for b in range(blocks):
            parts = split3(qkv[b, t, :HEAD_DIM, :].astype(F32) * (0.25 * LOG2E))
            qa[:48, b * lanes : (b + 1) * lanes] = jnp.concatenate(parts, axis=0)
        k = jnp.concatenate([qkv[0, t, HEAD_DIM:32, :], qkv[1, t, HEAD_DIM:32, :]], axis=1)
        k = jnp.concatenate([k, k, k], axis=0).T
        sample = jnp.dot(k, qa[:48, :], preferred_element_type=F32)
        shift = split3(-jnp.max(sample, axis=0, keepdims=True))
        row = lax.broadcasted_iota(jnp.int32, (16, nq), 0)
        rows = jnp.zeros((16, nq), F32)
        for i, part in enumerate(shift):
            rows = jnp.where(row == i, part.astype(F32), rows)
        qa[48:, :] = rows.astype(BF16)
        acc_ref[t] = absorb(t, qa[...], jnp.zeros((32, nq), F32), [qkv], ka, va)
        return carry

    lax.fori_loop(0, steps, step, 0)


def more_kernel(qa, acc_in, *refs):
    chunks, acc_out, ka, va = refs[:-3], refs[-3], refs[-2], refs[-1]

    def step(t, carry):
        acc_out[t] = absorb(t, qa[t], acc_in[t], chunks, ka, va)
        return carry

    lax.fori_loop(0, qa.shape[0], step, 0)


def end_kernel(count, qa, acc_in, qkv, *refs):
    chunks, out_ref, ka, va = refs[:-3], refs[-3], refs[-2], refs[-1]
    late = chunks[len(chunks) - count :]
    blocks, steps, _, lanes = qkv.shape
    nq = blocks * lanes

    def store(t, value):
        for b in range(blocks):
            out_ref[b, t] = value[:, b * lanes : (b + 1) * lanes].astype(BF16)

    def fast(t, bad):
        acc = absorb(t, qa[t], acc_in[t], late, ka, va)
        total = acc[HEAD_DIM : HEAD_DIM + 1]
        store(t, acc[:HEAD_DIM] / total)
        good = (total >= LOWEST) & (total <= HIGHEST)
        return jnp.maximum(bad, jnp.where(good, 0.0, 1.0))

    bad = lax.fori_loop(0, steps, fast, jnp.zeros((1, nq), F32))

    @pl.when(jnp.max(bad) > 0.0)
    def exact():
        one = jnp.ones((16, lanes), BF16)

        def step(t, carry):
            qq = jnp.concatenate([qkv[b, t, :HEAD_DIM, :] for b in range(blocks)], axis=1)

            def scores(chunk, i):
                k = chunk[i, t, -32:-HEAD_DIM].T
                return jnp.dot(k, qq, preferred_element_type=F32) * 0.25

            top = jnp.full((1, nq), -jnp.inf, F32)
            for chunk in (qkv, *chunks):

                def largest(i, top):
                    return jnp.maximum(top, jnp.max(scores(chunk, i), axis=0, keepdims=True))

                top = lax.fori_loop(0, blocks, largest, top)
            acc = jnp.zeros((32, nq), F32)
            for chunk in (qkv, *chunks):

                def block(i, acc):
                    p = jnp.exp(scores(chunk, i) - top).astype(BF16)
                    v = jnp.concatenate([chunk[i, t, -HEAD_DIM:], one], axis=0)
                    return acc + jnp.dot(v, p, preferred_element_type=F32)

                acc = lax.fori_loop(0, blocks, block, acc)
            store(t, acc[:HEAD_DIM] / acc[HEAD_DIM : HEAD_DIM + 1])
            return carry

        lax.fori_loop(0, steps, step, 0)


def attention(kernel, operands, out_shape, chunks, aliases={}):
    shape = operands[-1].shape
    near, steps, _, sens = shape
    keys = chunks * near * sens
    return pl.pallas_call(
        kernel,
        out_shape=out_shape,
        in_specs=[VMEM] * len(operands),
        out_specs=jax.tree.map(lambda _: VMEM, out_shape),
        scratch_shapes=[
            pltpu.VMEM((keys, 64), BF16),
            pltpu.VMEM((keys // 256, 32, 256), BF16),
        ],
        input_output_aliases=aliases,
        cost_estimate=pl.CostEstimate(
            flops=2 * keys * near * sens * steps * 256 * 2,
            bytes_accessed=0,
            transcendentals=keys * near * sens * steps,
        ),
        compiler_params=pltpu.CompilerParams(vmem_limit_bytes=48 << 20),
    )(*operands)


def last_kernel(mirror, attended, hidden, out_w, gain, out_ref):
    flip = mirror[0]
    heads, steps, dim, sens = attended.shape
    width = heads * dim
    for t in range(steps):
        rows = jnp.concatenate([attended[h ^ flip, t] for h in range(heads)], axis=0).T
        mixed = jnp.dot(rows, out_w[...], preferred_element_type=F32)
        mixed = mixed + hidden[t * sens : (t + 1) * sens, :].astype(F32)
        mean = jnp.mean(mixed, axis=-1, keepdims=True)
        centred = mixed - mean
        var = jnp.mean(centred * centred, axis=-1, keepdims=True)
        out_ref[t] = (centred / jnp.sqrt(var + 1e-5) * gain[...]).astype(BF16)


def local(series, conv_weight, qk_weight, value_weight, out_weight, norm_gain):
    steps, sens, width = series.shape
    blocks = lax.axis_size(TM)
    mirror = (lax.axis_index("y1") * 4 + lax.axis_index("x1") * 2).astype(jnp.int32).reshape(1)
    earlier = lax.ppermute(series[steps - 2 :], TM, [(i, i + 1) for i in range(blocks - 1)])
    hidden, qkv = pl.pallas_call(
        first_kernel,
        out_shape=(
            jax.ShapeDtypeStruct((steps * sens, width), BF16),
            jax.ShapeDtypeStruct((HEADS, steps, 3 * HEAD_DIM, sens), BF16),
        ),
        in_specs=[SMEM] + [VMEM] * 5,
        out_specs=(VMEM, VMEM),
        compiler_params=pltpu.CompilerParams(vmem_limit_bytes=32 << 20),
    )(mirror, earlier, series, conv_weight, qk_weight, value_weight)
    qkv = lax.all_to_all(qkv, NEAR, 0, 0, tiled=True)
    kv = qkv[:, :, HEAD_DIM:, :]

    def swap(block, mask):
        return lax.ppermute(block, SENSOR, [(i, i ^ mask) for i in range(64)])

    along_z, along_y, along_x = 0b000010, 0b110000, 0b001100
    from_z = swap(kv, along_z)
    from_y = swap(kv, along_y)
    from_x = swap(kv, along_x)
    from_xy = swap(kv, along_x | along_y)
    later = [swap(from_z, m) for m in (along_y, along_x, along_x | along_y)]
    near = qkv.shape[0]
    nq = near * sens
    state = (
        jax.ShapeDtypeStruct((steps, 64, nq), BF16),
        jax.ShapeDtypeStruct((steps, 32, nq), F32),
    )
    qa, acc = attention(begin_kernel, (qkv,), state, 1)
    acc = attention(more_kernel, (qa, acc, from_z, from_y), state[1], 2, {1: 0})
    acc = attention(more_kernel, (qa, acc, from_x, from_xy), state[1], 2, {1: 0})
    attended = attention(
        functools.partial(end_kernel, 3),
        (qa, acc, qkv, from_z, from_y, from_x, from_xy, *later),
        jax.ShapeDtypeStruct((near, steps, HEAD_DIM, sens), BF16),
        3,
    )
    attended = lax.all_to_all(attended, NEAR, 0, 0, tiled=True)
    return pl.pallas_call(
        last_kernel,
        out_shape=jax.ShapeDtypeStruct((steps, sens, width), BF16),
        in_specs=[SMEM] + [VMEM] * 4,
        out_specs=VMEM,
        compiler_params=pltpu.CompilerParams(vmem_limit_bytes=32 << 20),
    )(mirror, attended, hidden, out_weight, norm_gain.reshape(1, width))


def solution(mesh):
    fine = Mesh(mesh.devices.reshape((2,) * len(AXES)), AXES)
    spec = P(TM, SENSOR, None)
    return jax.shard_map(
        local,
        mesh=fine,
        in_specs=(spec, P(), P(), P(), P(), P()),
        out_specs=spec,
        check_vma=False,
    )
```

time: 165 us -> 199 us (1.21)
  Pallas kernels: 95.5 us -> 151 us
  waiting for transfers between devices: 16.7 us -> 7.59 us
  blocking collectives: 26.4 us -> 19.7 us
  starting transfers between devices: 21.1 us -> 17 us
    pallas_call x1 -> x4, Pallas kernels: 93.8 us -> 149 us  [attention(): pl.pallas_call(kernel, out_shape=out_shape, in_specs=[VMEM] * len(operand...]
    ppermute x7, waiting for transfers between devices: 9.09 us -> 0.03 us  [swap(): return lax.ppermute(block, SENSOR, [(i, i ^ mask) for i in range(64)])]
    all_to_all x1, blocking collectives: 13.3 us -> 8.48 us  [local(): attended = lax.all_to_all(attended, NEAR, 0, 0, tiled=True)]
    ppermute x7, starting transfers between devices: 19.2 us -> 15.1 us  [swap(): return lax.ppermute(block, SENSOR, [(i, i ^ mask) for i in range(64)])]
  transfers between devices with their start and end apart: 8 -> 8, of which waited for: 5 -> 1; matrix products, arithmetic and copies ran while one was open for 0% -> 0% of each run, Pallas kernels for 0% -> 8%
where the time goes in v2:
time: 199 us
  Pallas kernels  151 us (76%)
  blocking collectives  19.7 us (10%)
  starting transfers between devices  17 us (9%)
  waiting for transfers between devices  7.59 us (4%)
  local copies, waits for them, and re-layouts  3.36 us (2%)
    pallas_call x4, Pallas kernels, attention(): pl.pallas_call(kernel, out_shape=out_shape, in_specs=[VMEM] * len(operand...  149 us
    ppermute x7, starting transfers between devices, swap(): return lax.ppermute(block, SENSOR, [(i, i ^ mask) for i in range(64)])  15.1 us
    all_to_all x1, blocking collectives, local(): qkv = lax.all_to_all(qkv, NEAR, 0, 0, tiled=True)  11.2 us
    all_to_all x1, blocking collectives, local(): attended = lax.all_to_all(attended, NEAR, 0, 0, tiled=True)  8.48 us
    ppermute x1, waiting for transfers between devices, local(): lax.ppermute(series[steps - 2:], TM, [(i, i + 1) for i in range(blocks -...  7.56 us
  transfers between devices with their start and end apart: 8, of which 1 were waited for; matrix products, arithmetic and copies ran while one was open for 0% of the time, Pallas kernels for 8%

profile of v2, /device:TPU:192, one launch (start us, length us, event | category | flops | bytes accessed | tf_op | source)
XLA Modules:
  0.0 198.6 jit_solution(17262526772013075073)
XLA Ops:
  0.0 0.9 slice.6
  0.9 1.9 collective-permute-start
  2.8 7.6 %collective-permute-done.earlier = bf16[2,128,128]{2,1,0:T(8,128)(2,1)S(1)} collective-permute-done((bf16[2,128,128]{2,1,0:T(8,128)(2,1)S(1)}, bf16[2,128,128]{2,1,0:T(8,128)(2,1)S(1)}, u32[]{:S(2)}, u32[]{:S(2)}) %collective-permute-start) | collective-permute-done | bytes 65568 | tf_op jit(solution)/shard_map/ppermute | solution.py:200
  10.4 0.0 copy-done
  10.4 0.0 copy-done.3
  10.4 0.9 copy-done.1
  11.3 0.8 copy-done.2
  12.2 0.7 shard_map.64
  12.8 11.2 %all_to_all.10.qkv = bf16[8,3,48,128]{3,2,1,0:T(8,128)(2,1)S(1)} all-to-all(bf16[8,3,48,128]{3,2,1,0:T(8,128)(2,1)S(1)} %get-tuple-element.9), channel_id=1, replica_groups=mesh['y1'=2,'y0'=2,'x1'=2,'x0'=2,'z1'=2,'z0'=2,'zh'=2,'core'=2] {'y0','x..., dimensions={0} | all-to-all | bytes 589824 | tf_op jit(solution)/shard_map/all_to_all | solution.py:211
  24.0 3.2 %collective-permute-start.1 = (bf16[8,3,32,128]{3,2,1,0:T(8,128)(2,1)S(1)}, bf16[8,3,32,128]{3,2,1,0:T(8,128)(2,1)S(1)}, u32[]{:S(2)}, u32[]{:S(2)}) collective-permute-start(bf16[8,3,32,128]{3,2,1,0:T(8,128)(2,1)S(1)} %slice.8), channel_id=1, source_target_pairs={{0,8},{4,12},{8,0},{12,4},{16,24},{20,28},{24,16},{28,20},{32,40},... | collective-permute-start | bytes 589832 | tf_op jit(solution)/shard_map/ppermute | solution.py:215
  27.2 2.3 %collective-permute-start.2 = (bf16[8,3,32,128]{3,2,1,0:T(8,128)(2,1)S(1)}, bf16[8,3,32,128]{3,2,1,0:T(8,128)(2,1)S(1)}, u32[]{:S(2)}, u32[]{:S(2)}) collective-permute-start(bf16[8,3,32,128]{3,2,1,0:T(8,128)(2,1)S(1)} %slice.8), channel_id=1, source_target_pairs={{0,192},{4,196},{8,200},{12,204},{16,208},{20,212},{24,216},{28,22... | collective-permute-start | bytes 589832 | tf_op jit(solution)/shard_map/ppermute | solution.py:215
  29.5 1.9 collective-permute-start.3
  31.4 1.7 collective-permute-start.4
  33.1 3.8 %shard_map.65 = (bf16[3,64,1024]{2,1,0:T(8,128)(2,1)S(1)}, f32[3,32,1024]{2,1,0:T(8,128)S(1)}) custom-call(bf16[8,3,48,128]{3,2,1,0:T(8,128)(2,1)S(1)} %all_to_all.10.qkv), custom_call_target="tpu_custom_call" | custom-call | flops 3221225472 | tf_op jit(solution)/shard_map/pallas_call | solution.py:163
  36.9 0.0 collective-permute-done.1.refs_0_
  36.9 2.4 %collective-permute-start.5 = (bf16[8,3,32,128]{3,2,1,0:T(8,128)(2,1)S(1)}, bf16[8,3,32,128]{3,2,1,0:T(8,128)(2,1)S(1)}, u32[]{:S(2)}, u32[]{:S(2)}) collective-permute-start(bf16[8,3,32,128]{3,2,1,0:T(8,128)(2,1)S(1)} %collective-permute-done.1.refs_0_), channel_id=1, source_target_pairs={{0,192},{4,196},{8,200},{12,204},{16,208},{20,212},{24,216},{28,22... | collective-permute-start | bytes 589832 | tf_op jit(solution)/shard_map/ppermute | solution.py:215
  39.4 1.9 collective-permute-start.6
  41.2 0.0 collective-permute-done.2.refs_1_
  41.2 1.7 collective-permute-start.7
  42.9 6.0 %shard_map.66.acc_in = f32[3,32,1024]{2,1,0:T(8,128)S(1)} custom-call(bf16[3,64,1024]{2,1,0:T(8,128)(2,1)S(1)} %get-tuple-element.10.qa, f32[3,32,1024]{2,1,0:T(8,128)S(1)} %get-tuple-element.11.acc_in, bf16[8,3,32,128]{3,2,1,0:T(8,128)(2,1)S(1)} %collective-permute-done.1.refs_0_, ...), custom_call_target="tpu_custom_call", output_to_operand_aliasing={{}: (1, {})} | custom-call | flops 6442450944 | tf_op jit(solution)/shard_map/pallas_call | solution.py:163
  48.9 0.0 collective-permute-done.3.refs_0_.refs_2_
  48.9 0.0 collective-permute-done.4.refs_1_.refs_3_
  49.0 6.0 %shard_map.67.acc_in = f32[3,32,1024]{2,1,0:T(8,128)S(1)} custom-call(bf16[3,64,1024]{2,1,0:T(8,128)(2,1)S(1)} %get-tuple-element.10.qa, f32[3,32,1024]{2,1,0:T(8,128)S(1)} %shard_map.66.acc_in, bf16[8,3,32,128]{3,2,1,0:T(8,128)(2,1)S(1)} %collective-permute-done.3.refs_0_.refs_2_, ...), custom_call_target="tpu_custom_call", output_to_operand_aliasing={{}: (1, {})} | custom-call | flops 6442450944 | tf_op jit(solution)/shard_map/pallas_call | solution.py:163
  54.9 0.0 collective-permute-done.5.refs_4_
  54.9 0.0 collective-permute-done.6.refs_5_
  54.9 0.0 collective-permute-done.7.refs_6_
  55.0 133.4 %shard_map.68 = bf16[8,3,16,128]{3,2,1,0:T(8,128)(2,1)S(1)} custom-call(bf16[3,64,1024]{2,1,0:T(8,128)(2,1)S(1)} %get-tuple-element.10.qa, f32[3,32,1024]{2,1,0:T(8,128)S(1)} %shard_map.67.acc_in, bf16[8,3,48,128]{3,2,1,0:T(8,128)(2,1)S(1)} %all_to_all.10.qkv, bf16[8,3,32,128]{3,2,1,0:T(8,128)(2,1)S(1)} %collective-permute-done.1.refs_0_, ...), custom_call_target="tpu_custom_call" | custom-call | flops 9663676416 | tf_op jit(solution)/shard_map/pallas_call | solution.py:163
  188.4 0.0 copy-start.4
  188.4 8.5 %all_to_all.11.attended = bf16[8,3,16,128]{3,2,1,0:T(8,128)(2,1)S(1)} all-to-all(bf16[8,3,16,128]{3,2,1,0:T(8,128)(2,1)S(1)} %shard_map.68), channel_id=1, replica_groups=mesh['y1'=2,'y0'=2,'x1'=2,'x0'=2,'z1'=2,'z0'=2,'zh'=2,'core'=2] {'y0','x..., dimensions={0} | all-to-all | bytes 196608 | tf_op jit(solution)/shard_map/all_to_all | solution.py:238
  196.9 0.0 copy-done.4
  196.9 0.7 copy-done.5
  197.5 1.1 shard_map.69
  (6 shorter events, 0.0 us)
Async XLA Ops:
  0.0 10.4 %copy-start = (bf16[3,128,128]{2,1,0:T(8,128)(2,1)S(1)}, bf16[3,128,128]{2,1,0:T(8,128)(2,1)}, u32[]{:S(2)}) copy-start(bf16[3,128,128]{2,1,0:T(8,128)(2,1)} %series.1) | copy-start | bytes 294916
  0.0 10.4 %copy-start.3 = (bf16[128,128]{1,0:T(8,128)(2,1)S(1)}, bf16[128,128]{1,0:T(8,128)(2,1)}, u32[]{:S(2)}) copy-start(bf16[128,128]{1,0:T(8,128)(2,1)} %value_w.1) | copy-start | bytes 98308
  0.9 9.5 %collective-permute-start = (bf16[2,128,128]{2,1,0:T(8,128)(2,1)S(1)}, bf16[2,128,128]{2,1,0:T(8,128)(2,1)S(1)}, u32[]{:S(2)}, u32[]{:S(2)}) collective-permute-start(bf16[2,128,128]{2,1,0:T(8,128)(2,1)S(1)} %slice.6), channel_id=1, source_target_pairs={{0,1},{1,2},{2,3},{4,5},{5,6},{6,7},{8,9},{9,10},{10,11},{12,13},{... | collective-permute-start | bytes 196616 | tf_op jit(solution)/shard_map/ppermute | solution.py:200
  10.4 0.9 copy-start.1
  11.3 0.8 copy-start.2
  24.0 12.9 %collective-permute-start.1 = (bf16[8,3,32,128]{3,2,1,0:T(8,128)(2,1)S(1)}, bf16[8,3,32,128]{3,2,1,0:T(8,128)(2,1)S(1)}, u32[]{:S(2)}, u32[]{:S(2)}) collective-permute-start(bf16[8,3,32,128]{3,2,1,0:T(8,128)(2,1)S(1)} %slice.8), channel_id=1, source_target_pairs={{0,8},{4,12},{8,0},{12,4},{16,24},{20,28},{24,16},{28,20},{32,40},... | collective-permute-start | bytes 589832 | tf_op jit(solution)/shard_map/ppermute | solution.py:215
  27.2 14.0 %collective-permute-start.2 = (bf16[8,3,32,128]{3,2,1,0:T(8,128)(2,1)S(1)}, bf16[8,3,32,128]{3,2,1,0:T(8,128)(2,1)S(1)}, u32[]{:S(2)}, u32[]{:S(2)}) collective-permute-start(bf16[8,3,32,128]{3,2,1,0:T(8,128)(2,1)S(1)} %slice.8), channel_id=1, source_target_pairs={{0,192},{4,196},{8,200},{12,204},{16,208},{20,212},{24,216},{28,22... | collective-permute-start | bytes 589832 | tf_op jit(solution)/shard_map/ppermute | solution.py:215
  29.5 19.4 %collective-permute-start.3 = (bf16[8,3,32,128]{3,2,1,0:T(8,128)(2,1)S(1)}, bf16[8,3,32,128]{3,2,1,0:T(8,128)(2,1)S(1)}, u32[]{:S(2)}, u32[]{:S(2)}) collective-permute-start(bf16[8,3,32,128]{3,2,1,0:T(8,128)(2,1)S(1)} %slice.8), channel_id=1, source_target_pairs={{0,48},{4,52},{8,56},{12,60},{16,32},{20,36},{24,40},{28,44},{32,1... | collective-permute-start | bytes 589832 | tf_op jit(solution)/shard_map/ppermute | solution.py:215
  31.4 17.5 %collective-permute-start.4 = (bf16[8,3,32,128]{3,2,1,0:T(8,128)(2,1)S(1)}, bf16[8,3,32,128]{3,2,1,0:T(8,128)(2,1)S(1)}, u32[]{:S(2)}, u32[]{:S(2)}) collective-permute-start(bf16[8,3,32,128]{3,2,1,0:T(8,128)(2,1)S(1)} %slice.8), channel_id=1, source_target_pairs={{0,240},{4,244},{8,248},{12,252},{16,224},{20,228},{24,232},{28,23... | collective-permute-start | bytes 589832 | tf_op jit(solution)/shard_map/ppermute | solution.py:215
  36.9 18.0 %collective-permute-start.5 = (bf16[8,3,32,128]{3,2,1,0:T(8,128)(2,1)S(1)}, bf16[8,3,32,128]{3,2,1,0:T(8,128)(2,1)S(1)}, u32[]{:S(2)}, u32[]{:S(2)}) collective-permute-start(bf16[8,3,32,128]{3,2,1,0:T(8,128)(2,1)S(1)} %collective-permute-done.1.refs_0_), channel_id=1, source_target_pairs={{0,192},{4,196},{8,200},{12,204},{16,208},{20,212},{24,216},{28,22... | collective-permute-start | bytes 589832 | tf_op jit(solution)/shard_map/ppermute | solution.py:215
  39.4 15.6 %collective-permute-start.6 = (bf16[8,3,32,128]{3,2,1,0:T(8,128)(2,1)S(1)}, bf16[8,3,32,128]{3,2,1,0:T(8,128)(2,1)S(1)}, u32[]{:S(2)}, u32[]{:S(2)}) collective-permute-start(bf16[8,3,32,128]{3,2,1,0:T(8,128)(2,1)S(1)} %collective-permute-done.1.refs_0_), channel_id=1, source_target_pairs={{0,48},{4,52},{8,56},{12,60},{16,32},{20,36},{24,40},{28,44},{32,1... | collective-permute-start | bytes 589832 | tf_op jit(solution)/shard_map/ppermute | solution.py:215
  41.2 13.7 %collective-permute-start.7 = (bf16[8,3,32,128]{3,2,1,0:T(8,128)(2,1)S(1)}, bf16[8,3,32,128]{3,2,1,0:T(8,128)(2,1)S(1)}, u32[]{:S(2)}, u32[]{:S(2)}) collective-permute-start(bf16[8,3,32,128]{3,2,1,0:T(8,128)(2,1)S(1)} %collective-permute-done.1.refs_0_), channel_id=1, source_target_pairs={{0,240},{4,244},{8,248},{12,252},{16,224},{20,228},{24,232},{28,23... | collective-permute-start | bytes 589832 | tf_op jit(solution)/shard_map/ppermute | solution.py:215
  188.4 8.5 %copy-start.4 = (bf16[128,128]{1,0:T(8,128)(2,1)S(1)}, bf16[128,128]{1,0:T(8,128)(2,1)}, u32[]{:S(2)}) copy-start(bf16[128,128]{1,0:T(8,128)(2,1)} %out_w.1) | copy-start | bytes 98308
  196.9 0.7 copy-start.5

commit v3 on v2

--- a/solution.py
+++ b/solution.py
@@ -18,6 +18,7 @@
 NEAR = ("y0", "x0", "z0")
 VMEM = pl.BlockSpec(memory_space=pltpu.VMEM)
 SMEM = pl.BlockSpec(memory_space=pltpu.SMEM)
+TILE = 512
 LOWEST = 2.0**-20
 HIGHEST = 2.0**100
 
@@ -30,15 +31,26 @@
     return high, mid, low
 
 
-def first_kernel(mirror, earlier, series, conv_w, qk_w, value_w, hidden_ref, qkv_ref):
+def early_kernel(series, conv_w, gain, conv_ref, gain_ref):
+    steps, sens, width = series.shape
+    own = series[...].reshape(steps * sens, width)
+    conv_ref[...] = jnp.dot(own, conv_w[0], preferred_element_type=F32)
+    for tap in (1, 2):
+        rows = (steps - tap) * sens
+        conv_ref[tap * sens :, :] += jnp.dot(own[:rows], conv_w[tap], preferred_element_type=F32)
+    gain_ref[...] = gain[...]
+
+
+def first_kernel(mirror, earlier, series, conv_own, conv_w, qk_w, value_w, hidden_ref, qkv_ref):
     flip = mirror[0]
     steps, sens, width = series.shape
     own = series[...].reshape(steps * sens, width)
-    padded = jnp.concatenate([earlier[...].reshape(2 * sens, width), own], axis=0)
-    conv = jnp.dot(own, conv_w[0], preferred_element_type=F32)
-    for tap in (1, 2):
-        window = padded[(2 - tap) * sens : (2 - tap + steps) * sens]
-        conv = conv + jnp.dot(window, conv_w[tap], preferred_element_type=F32)
+    before = earlier[steps - 2 :].reshape(2 * sens, width)
+    late = jnp.dot(before, conv_w[2], preferred_element_type=F32)
+    near = jnp.dot(before[sens:], conv_w[1], preferred_element_type=F32)
+    late = late + jnp.concatenate([near, jnp.zeros_like(near)], axis=0)
+    conv = conv_own[...]
+    conv = jnp.concatenate([conv[: 2 * sens] + late, conv[2 * sens :]], axis=0)
     gate = jax.nn.sigmoid(conv[:, width:])
     hidden = (own.astype(F32) + conv[:, :width] * gate).astype(BF16)
     hidden_ref[...] = hidden
@@ -63,18 +75,23 @@
             ka[pair * 256 : (pair + 1) * 256, :] = jnp.concatenate([k, k, k, one], axis=0).T
             va[pair] = jnp.concatenate([kv[HEAD_DIM:], one], axis=0)
     pairs = len(chunks) * (blocks // 2)
-    s = jnp.dot(ka[: pairs * 256, :], qq, preferred_element_type=F32)
-    p = jnp.exp2(s).astype(BF16)
-    for u in range(pairs):
-        acc = acc + jnp.dot(va[u], p[u * 256 : (u + 1) * 256], preferred_element_type=F32)
-    return acc
+    sums = []
+    for start in range(0, acc.shape[1], TILE):
+        cut = slice(start, start + TILE)
+        s = jnp.dot(ka[: pairs * 256, :], qq[:, cut], preferred_element_type=F32)
+        p = jnp.exp2(s).astype(BF16)
+        part = acc[:, cut]
+        for u in range(pairs):
+            part = part + jnp.dot(va[u], p[u * 256 : (u + 1) * 256], preferred_element_type=F32)
+        sums.append(part)
+    return jnp.concatenate(sums, axis=1)
 
 
 def begin_kernel(qkv, qa_ref, acc_ref, ka, va):
     blocks, steps, _, lanes = qkv.shape
     nq = blocks * lanes
 
-    def step(t, carry):
+    for t in range(steps):
         qa = qa_ref.at[t]
         for b in range(blocks):
             parts = split3(qkv[b, t, :HEAD_DIM, :].astype(F32) * (0.25 * LOG2E))
@@ -88,20 +105,14 @@
         for i, part in enumerate(shift):
             rows = jnp.where(row == i, part.astype(F32), rows)
         qa[48:, :] = rows.astype(BF16)
-        acc_ref[t] = absorb(t, qa[...], jnp.zeros((32, nq), F32), [qkv], ka, va)
-        return carry
-
-    lax.fori_loop(0, steps, step, 0)
+        acc_ref[t] = absorb(t, qa[...], jnp.zeros((32, nq), F32), [qkv], ka.at[t], va.at[t])
 
 
 def more_kernel(qa, acc_in, *refs):
     chunks, acc_out, ka, va = refs[:-3], refs[-3], refs[-2], refs[-1]
 
-    def step(t, carry):
-        acc_out[t] = absorb(t, qa[t], acc_in[t], chunks, ka, va)
-        return carry
-
-    lax.fori_loop(0, qa.shape[0], step, 0)
+    for t in range(qa.shape[0]):
+        acc_out[t] = absorb(t, qa[t], acc_in[t], chunks, ka.at[t], va.at[t])
 
 
 def end_kernel(count, qa, acc_in, qkv, *refs):
@@ -114,14 +125,13 @@
         for b in range(blocks):
             out_ref[b, t] = value[:, b * lanes : (b + 1) * lanes].astype(BF16)
 
-    def fast(t, bad):
-        acc = absorb(t, qa[t], acc_in[t], late, ka, va)
+    bad = jnp.zeros((1, nq), F32)
+    for t in range(steps):
+        acc = absorb(t, qa[t], acc_in[t], late, ka.at[t], va.at[t])
         total = acc[HEAD_DIM : HEAD_DIM + 1]
         store(t, acc[:HEAD_DIM] / total)
         good = (total >= LOWEST) & (total <= HIGHEST)
-        return jnp.maximum(bad, jnp.where(good, 0.0, 1.0))
-
-    bad = lax.fori_loop(0, steps, fast, jnp.zeros((1, nq), F32))
+        bad = jnp.maximum(bad, jnp.where(good, 0.0, 1.0))
 
     @pl.when(jnp.max(bad) > 0.0)
     def exact():
@@ -166,8 +176,8 @@
         in_specs=[VMEM] * len(operands),
         out_specs=jax.tree.map(lambda _: VMEM, out_shape),
         scratch_shapes=[
-            pltpu.VMEM((keys, 64), BF16),
-            pltpu.VMEM((keys // 256, 32, 256), BF16),
+            pltpu.VMEM((steps, keys, 64), BF16),
+            pltpu.VMEM((steps, keys // 256, 32, 256), BF16),
         ],
         input_output_aliases=aliases,
         cost_estimate=pl.CostEstimate(
@@ -197,17 +207,30 @@
     steps, sens, width = series.shape
     blocks = lax.axis_size(TM)
     mirror = (lax.axis_index("y1") * 4 + lax.axis_index("x1") * 2).astype(jnp.int32).reshape(1)
-    earlier = lax.ppermute(series[steps - 2 :], TM, [(i, i + 1) for i in range(blocks - 1)])
+    earlier = lax.ppermute(series, TM, [(i, i + 1) for i in range(blocks - 1)])
+    conv_own, gain = pl.pallas_call(
+        early_kernel,
+        out_shape=(
+            jax.ShapeDtypeStruct((steps * sens, 2 * width), F32),
+            jax.ShapeDtypeStruct((1, width), F32),
+        ),
+        in_specs=[VMEM] * 3,
+        out_specs=(VMEM, VMEM),
+        cost_estimate=pl.CostEstimate(
+            flops=2 * 3 * steps * sens * width * 2 * width, bytes_accessed=0, transcendentals=0
+        ),
+        compiler_params=pltpu.CompilerParams(vmem_limit_bytes=32 << 20),
+    )(series, conv_weight, norm_gain.reshape(1, width))
     hidden, qkv = pl.pallas_call(
         first_kernel,
         out_shape=(
             jax.ShapeDtypeStruct((steps * sens, width), BF16),
             jax.ShapeDtypeStruct((HEADS, steps, 3 * HEAD_DIM, sens), BF16),
         ),
-        in_specs=[SMEM] + [VMEM] * 5,
+        in_specs=[SMEM] + [VMEM] * 6,
         out_specs=(VMEM, VMEM),
         compiler_params=pltpu.CompilerParams(vmem_limit_bytes=32 << 20),
-    )(mirror, earlier, series, conv_weight, qk_weight, value_weight)
+    )(mirror, earlier, series, conv_own, conv_weight, qk_weight, value_weight)
     qkv = lax.all_to_all(qkv, NEAR, 0, 0, tiled=True)
     kv = qkv[:, :, HEAD_DIM:, :]
 
@@ -242,7 +265,7 @@
         in_specs=[SMEM] + [VMEM] * 4,
         out_specs=VMEM,
         compiler_params=pltpu.CompilerParams(vmem_limit_bytes=32 << 20),
-    )(mirror, attended, hidden, out_weight, norm_gain.reshape(1, width))
+    )(mirror, attended, hidden, out_weight, gain)
 
 
 def solution(mesh):

time: 199 us -> 195 us (0.980)
  no operation moved by 1% of the time
where the time goes in v3:
time: 195 us
  Pallas kernels  150 us (77%)
  blocking collectives  19.2 us (10%)
  starting transfers between devices  17.1 us (9%)
  waiting for transfers between devices  6.45 us (3%)
  local copies, waits for them, and re-layouts  2.49 us (1%)
    pallas_call x4, Pallas kernels, attention(): pl.pallas_call(kernel, out_shape=out_shape, in_specs=[VMEM] * len(operand...  148 us
    ppermute x7, starting transfers between devices, swap(): return lax.ppermute(block, SENSOR, [(i, i ^ mask) for i in range(64)])  15.2 us
    all_to_all x1, blocking collectives, local(): qkv = lax.all_to_all(qkv, NEAR, 0, 0, tiled=True)  10.7 us
    all_to_all x1, blocking collectives, local(): attended = lax.all_to_all(attended, NEAR, 0, 0, tiled=True)  8.48 us
    ppermute x1, waiting for transfers between devices, local(): earlier = lax.ppermute(series, TM, [(i, i + 1) for i in range(blocks - 1)])  6.44 us
  transfers between devices with their start and end apart: 8, of which 1 were waited for; matrix products, arithmetic and copies ran while one was open for 0% of the time, Pallas kernels for 8%

profile of v3, /device:TPU:192, one launch (start us, length us, event | category | flops | bytes accessed | tf_op | source)
XLA Modules:
  0.0 195.1 jit_solution(1406770534430637652)
XLA Ops:
  0.0 1.9 collective-permute-start
  1.9 0.0 copy-start.5
  1.9 0.6 copy-done.5
  2.6 0.9 copy-done
  3.5 0.9 copy-done.1
  4.4 0.2 shard_map.64
  4.7 6.4 %collective-permute-done.earlier = bf16[3,128,128]{2,1,0:T(8,128)(2,1)S(1)} collective-permute-done((bf16[3,128,128]{2,1,0:T(8,128)(2,1)}, bf16[3,128,128]{2,1,0:T(8,128)(2,1)S(1)}, u32[]{:S(2)}, u32[]{:S(2)}) %collective-permute-start) | collective-permute-done | bytes 98336 | tf_op jit(solution)/shard_map/ppermute | solution.py:210
  11.1 0.0 copy-done.2
  11.1 0.5 shard_map.65
  11.6 10.7 %all_to_all.10.qkv = bf16[8,3,48,128]{3,2,1,0:T(8,128)(2,1)S(1)} all-to-all(bf16[8,3,48,128]{3,2,1,0:T(8,128)(2,1)S(1)} %get-tuple-element.12), channel_id=1, replica_groups=mesh['y1'=2,'y0'=2,'x1'=2,'x0'=2,'z1'=2,'z0'=2,'zh'=2,'core'=2] {'y0','x..., dimensions={0} | all-to-all | bytes 589824 | tf_op jit(solution)/shard_map/all_to_all | solution.py:234
  22.4 3.3 %collective-permute-start.1 = (bf16[8,3,32,128]{3,2,1,0:T(8,128)(2,1)S(1)}, bf16[8,3,32,128]{3,2,1,0:T(8,128)(2,1)S(1)}, u32[]{:S(2)}, u32[]{:S(2)}) collective-permute-start(bf16[8,3,32,128]{3,2,1,0:T(8,128)(2,1)S(1)} %slice.4), channel_id=1, source_target_pairs={{0,8},{4,12},{8,0},{12,4},{16,24},{20,28},{24,16},{28,20},{32,40},... | collective-permute-start | bytes 589832 | tf_op jit(solution)/shard_map/ppermute | solution.py:238
  25.7 2.7 %collective-permute-start.2 = (bf16[8,3,32,128]{3,2,1,0:T(8,128)(2,1)S(1)}, bf16[8,3,32,128]{3,2,1,0:T(8,128)(2,1)S(1)}, u32[]{:S(2)}, u32[]{:S(2)}) collective-permute-start(bf16[8,3,32,128]{3,2,1,0:T(8,128)(2,1)S(1)} %slice.4), channel_id=1, source_target_pairs={{0,192},{4,196},{8,200},{12,204},{16,208},{20,212},{24,216},{28,22... | collective-permute-start | bytes 589832 | tf_op jit(solution)/shard_map/ppermute | solution.py:238
  28.3 1.9 collective-permute-start.3
  30.2 1.4 collective-permute-start.4
  31.6 3.5 %shard_map.66 = (bf16[3,64,1024]{2,1,0:T(8,128)(2,1)S(1)}, f32[3,32,1024]{2,1,0:T(8,128)S(1)}) custom-call(bf16[8,3,48,128]{3,2,1,0:T(8,128)(2,1)S(1)} %all_to_all.10.qkv), custom_call_target="tpu_custom_call" | custom-call | flops 3221225472 | tf_op jit(solution)/shard_map/pallas_call | solution.py:173
  35.1 0.0 collective-permute-done.1.refs_0_
  35.1 2.7 %collective-permute-start.5 = (bf16[8,3,32,128]{3,2,1,0:T(8,128)(2,1)S(1)}, bf16[8,3,32,128]{3,2,1,0:T(8,128)(2,1)S(1)}, u32[]{:S(2)}, u32[]{:S(2)}) collective-permute-start(bf16[8,3,32,128]{3,2,1,0:T(8,128)(2,1)S(1)} %collective-permute-done.1.refs_0_), channel_id=1, source_target_pairs={{0,192},{4,196},{8,200},{12,204},{16,208},{20,212},{24,216},{28,22... | collective-permute-start | bytes 589832 | tf_op jit(solution)/shard_map/ppermute | solution.py:238
  37.8 1.9 collective-permute-start.6
  39.7 0.0 collective-permute-done.2.refs_1_
  39.7 1.4 collective-permute-start.7
  41.1 5.5 %shard_map.67.acc_in = f32[3,32,1024]{2,1,0:T(8,128)S(1)} custom-call(bf16[3,64,1024]{2,1,0:T(8,128)(2,1)S(1)} %get-tuple-element.13.qa, f32[3,32,1024]{2,1,0:T(8,128)S(1)} %get-tuple-element.14.acc_in, bf16[8,3,32,128]{3,2,1,0:T(8,128)(2,1)S(1)} %collective-permute-done.1.refs_0_, ...), custom_call_target="tpu_custom_call", output_to_operand_aliasing={{}: (1, {})} | custom-call | flops 6442450944 | tf_op jit(solution)/shard_map/pallas_call | solution.py:173
  46.6 0.0 collective-permute-done.3.refs_0_.refs_2_
  46.6 0.0 collective-permute-done.4.refs_1_.refs_3_
  46.6 5.5 %shard_map.68.acc_in = f32[3,32,1024]{2,1,0:T(8,128)S(1)} custom-call(bf16[3,64,1024]{2,1,0:T(8,128)(2,1)S(1)} %get-tuple-element.13.qa, f32[3,32,1024]{2,1,0:T(8,128)S(1)} %shard_map.67.acc_in, bf16[8,3,32,128]{3,2,1,0:T(8,128)(2,1)S(1)} %collective-permute-done.3.refs_0_.refs_2_, ...), custom_call_target="tpu_custom_call", output_to_operand_aliasing={{}: (1, {})} | custom-call | flops 6442450944 | tf_op jit(solution)/shard_map/pallas_call | solution.py:173
  52.1 0.0 collective-permute-done.5.refs_4_
  52.1 0.0 collective-permute-done.6.refs_5_
  52.2 0.0 collective-permute-done.7.refs_6_
  52.2 133.4 %shard_map.69 = bf16[8,3,16,128]{3,2,1,0:T(8,128)(2,1)S(1)} custom-call(bf16[3,64,1024]{2,1,0:T(8,128)(2,1)S(1)} %get-tuple-element.13.qa, f32[3,32,1024]{2,1,0:T(8,128)S(1)} %shard_map.68.acc_in, bf16[8,3,48,128]{3,2,1,0:T(8,128)(2,1)S(1)} %all_to_all.10.qkv, bf16[8,3,32,128]{3,2,1,0:T(8,128)(2,1)S(1)} %collective-permute-done.1.refs_0_, ...), custom_call_target="tpu_custom_call" | custom-call | flops 9663676416 | tf_op jit(solution)/shard_map/pallas_call | solution.py:173
  185.6 0.0 copy-start.4
  185.6 8.5 %all_to_all.11.attended = bf16[8,3,16,128]{3,2,1,0:T(8,128)(2,1)S(1)} all-to-all(bf16[8,3,16,128]{3,2,1,0:T(8,128)(2,1)S(1)} %shard_map.69), channel_id=1, replica_groups=mesh['y1'=2,'y0'=2,'x1'=2,'x0'=2,'z1'=2,'z0'=2,'zh'=2,'core'=2] {'y0','x..., dimensions={0} | all-to-all | bytes 196608 | tf_op jit(solution)/shard_map/all_to_all | solution.py:261
  194.1 0.0 copy-done.4
  194.1 1.1 shard_map.70
  (6 shorter events, 0.0 us)
Async XLA Ops:
  0.0 11.1 %collective-permute-start = (bf16[3,128,128]{2,1,0:T(8,128)(2,1)}, bf16[3,128,128]{2,1,0:T(8,128)(2,1)S(1)}, u32[]{:S(2)}, u32[]{:S(2)}) collective-permute-start(bf16[3,128,128]{2,1,0:T(8,128)(2,1)} %series.3), channel_id=1, source_target_pairs={{0,1},{1,2},{2,3},{4,5},{5,6},{6,7},{8,9},{9,10},{10,11},{12,13},{... | collective-permute-start | bytes 294920 | tf_op jit(solution)/shard_map/ppermute | solution.py:210
  1.9 0.7 copy-start.5
  2.6 0.9 copy-start
  3.5 0.9 copy-start.1
  4.4 6.7 %copy-start.2 = (bf16[2,128,128]{2,1,0:T(8,128)(2,1)S(1)}, bf16[2,128,128]{2,1,0:T(8,128)(2,1)}, u32[]{:S(2)}) copy-start(bf16[2,128,128]{2,1,0:T(8,128)(2,1)} %qk_w.1) | copy-start | bytes 196612
  4.4 6.7 %copy-start.3 = (bf16[128,128]{1,0:T(8,128)(2,1)S(1)}, bf16[128,128]{1,0:T(8,128)(2,1)}, u32[]{:S(2)}) copy-start(bf16[128,128]{1,0:T(8,128)(2,1)} %value_w.1) | copy-start | bytes 98308
  22.4 12.7 %collective-permute-start.1 = (bf16[8,3,32,128]{3,2,1,0:T(8,128)(2,1)S(1)}, bf16[8,3,32,128]{3,2,1,0:T(8,128)(2,1)S(1)}, u32[]{:S(2)}, u32[]{:S(2)}) collective-permute-start(bf16[8,3,32,128]{3,2,1,0:T(8,128)(2,1)S(1)} %slice.4), channel_id=1, source_target_pairs={{0,8},{4,12},{8,0},{12,4},{16,24},{20,28},{24,16},{28,20},{32,40},... | collective-permute-start | bytes 589832 | tf_op jit(solution)/shard_map/ppermute | solution.py:238
  25.7 14.0 %collective-permute-start.2 = (bf16[8,3,32,128]{3,2,1,0:T(8,128)(2,1)S(1)}, bf16[8,3,32,128]{3,2,1,0:T(8,128)(2,1)S(1)}, u32[]{:S(2)}, u32[]{:S(2)}) collective-permute-start(bf16[8,3,32,128]{3,2,1,0:T(8,128)(2,1)S(1)} %slice.4), channel_id=1, source_target_pairs={{0,192},{4,196},{8,200},{12,204},{16,208},{20,212},{24,216},{28,22... | collective-permute-start | bytes 589832 | tf_op jit(solution)/shard_map/ppermute | solution.py:238
  28.3 18.3 %collective-permute-start.3 = (bf16[8,3,32,128]{3,2,1,0:T(8,128)(2,1)S(1)}, bf16[8,3,32,128]{3,2,1,0:T(8,128)(2,1)S(1)}, u32[]{:S(2)}, u32[]{:S(2)}) collective-permute-start(bf16[8,3,32,128]{3,2,1,0:T(8,128)(2,1)S(1)} %slice.4), channel_id=1, source_target_pairs={{0,48},{4,52},{8,56},{12,60},{16,32},{20,36},{24,40},{28,44},{32,1... | collective-permute-start | bytes 589832 | tf_op jit(solution)/shard_map/ppermute | solution.py:238
  30.2 16.4 %collective-permute-start.4 = (bf16[8,3,32,128]{3,2,1,0:T(8,128)(2,1)S(1)}, bf16[8,3,32,128]{3,2,1,0:T(8,128)(2,1)S(1)}, u32[]{:S(2)}, u32[]{:S(2)}) collective-permute-start(bf16[8,3,32,128]{3,2,1,0:T(8,128)(2,1)S(1)} %slice.4), channel_id=1, source_target_pairs={{0,240},{4,244},{8,248},{12,252},{16,224},{20,228},{24,232},{28,23... | collective-permute-start | bytes 589832 | tf_op jit(solution)/shard_map/ppermute | solution.py:238
  35.1 17.0 %collective-permute-start.5 = (bf16[8,3,32,128]{3,2,1,0:T(8,128)(2,1)S(1)}, bf16[8,3,32,128]{3,2,1,0:T(8,128)(2,1)S(1)}, u32[]{:S(2)}, u32[]{:S(2)}) collective-permute-start(bf16[8,3,32,128]{3,2,1,0:T(8,128)(2,1)S(1)} %collective-permute-done.1.refs_0_), channel_id=1, source_target_pairs={{0,192},{4,196},{8,200},{12,204},{16,208},{20,212},{24,216},{28,22... | collective-permute-start | bytes 589832 | tf_op jit(solution)/shard_map/ppermute | solution.py:238
  37.8 14.3 %collective-permute-start.6 = (bf16[8,3,32,128]{3,2,1,0:T(8,128)(2,1)S(1)}, bf16[8,3,32,128]{3,2,1,0:T(8,128)(2,1)S(1)}, u32[]{:S(2)}, u32[]{:S(2)}) collective-permute-start(bf16[8,3,32,128]{3,2,1,0:T(8,128)(2,1)S(1)} %collective-permute-done.1.refs_0_), channel_id=1, source_target_pairs={{0,48},{4,52},{8,56},{12,60},{16,32},{20,36},{24,40},{28,44},{32,1... | collective-permute-start | bytes 589832 | tf_op jit(solution)/shard_map/ppermute | solution.py:238
  39.7 12.4 %collective-permute-start.7 = (bf16[8,3,32,128]{3,2,1,0:T(8,128)(2,1)S(1)}, bf16[8,3,32,128]{3,2,1,0:T(8,128)(2,1)S(1)}, u32[]{:S(2)}, u32[]{:S(2)}) collective-permute-start(bf16[8,3,32,128]{3,2,1,0:T(8,128)(2,1)S(1)} %collective-permute-done.1.refs_0_), channel_id=1, source_target_pairs={{0,240},{4,244},{8,248},{12,252},{16,224},{20,228},{24,232},{28,23... | collective-permute-start | bytes 589832 | tf_op jit(solution)/shard_map/ppermute | solution.py:238
  185.6 8.5 %copy-start.4 = (bf16[128,128]{1,0:T(8,128)(2,1)S(1)}, bf16[128,128]{1,0:T(8,128)(2,1)}, u32[]{:S(2)}) copy-start(bf16[128,128]{1,0:T(8,128)(2,1)} %out_w.1) | copy-start | bytes 98308

commit v4 on v3

--- a/solution.py
+++ b/solution.py
@@ -19,6 +19,7 @@
 VMEM = pl.BlockSpec(memory_space=pltpu.VMEM)
 SMEM = pl.BlockSpec(memory_space=pltpu.SMEM)
 TILE = 512
+ROWS = HEAD_DIM + 8
 LOWEST = 2.0**-20
 HIGHEST = 2.0**100
 
@@ -45,7 +46,7 @@
     flip = mirror[0]
     steps, sens, width = series.shape
     own = series[...].reshape(steps * sens, width)
-    before = earlier[steps - 2 :].reshape(2 * sens, width)
+    before = earlier[...].reshape(2 * sens, width)
     late = jnp.dot(before, conv_w[2], preferred_element_type=F32)
     near = jnp.dot(before[sens:], conv_w[1], preferred_element_type=F32)
     late = late + jnp.concatenate([near, jnp.zeros_like(near)], axis=0)
@@ -73,18 +74,22 @@
             k = kv[:HEAD_DIM]
             pair = c * (blocks // 2) + p
             ka[pair * 256 : (pair + 1) * 256, :] = jnp.concatenate([k, k, k, one], axis=0).T
-            va[pair] = jnp.concatenate([kv[HEAD_DIM:], one], axis=0)
+            va[pair] = kv[HEAD_DIM:]
     pairs = len(chunks) * (blocks // 2)
-    sums = []
+    parts = []
     for start in range(0, acc.shape[1], TILE):
         cut = slice(start, start + TILE)
         s = jnp.dot(ka[: pairs * 256, :], qq[:, cut], preferred_element_type=F32)
-        p = jnp.exp2(s).astype(BF16)
-        part = acc[:, cut]
+        probs = jnp.exp2(s)
+        total = acc[HEAD_DIM:, cut] + jnp.sum(probs.reshape(pairs * 32, 8, TILE), axis=0)
+        probs = probs.astype(BF16)
+        out = acc[:HEAD_DIM, cut]
         for u in range(pairs):
-            part = part + jnp.dot(va[u], p[u * 256 : (u + 1) * 256], preferred_element_type=F32)
-        sums.append(part)
-    return jnp.concatenate(sums, axis=1)
+            out = out + jnp.dot(
+                va[u], probs[u * 256 : (u + 1) * 256], preferred_element_type=F32
+            )
+        parts.append(jnp.concatenate([out, total], axis=0))
+    return jnp.concatenate(parts, axis=1)
 
 
 def begin_kernel(qkv, qa_ref, acc_ref, ka, va):
@@ -105,7 +110,7 @@
         for i, part in enumerate(shift):
             rows = jnp.where(row == i, part.astype(F32), rows)
         qa[48:, :] = rows.astype(BF16)
-        acc_ref[t] = absorb(t, qa[...], jnp.zeros((32, nq), F32), [qkv], ka.at[t], va.at[t])
+        acc_ref[t] = absorb(t, qa[...], jnp.zeros((ROWS, nq), F32), [qkv], ka.at[t], va.at[t])
 
 
 def more_kernel(qa, acc_in, *refs):
@@ -128,15 +133,13 @@
     bad = jnp.zeros((1, nq), F32)
     for t in range(steps):
         acc = absorb(t, qa[t], acc_in[t], late, ka.at[t], va.at[t])
-        total = acc[HEAD_DIM : HEAD_DIM + 1]
+        total = jnp.sum(acc[HEAD_DIM:], axis=0, keepdims=True)
         store(t, acc[:HEAD_DIM] / total)
         good = (total >= LOWEST) & (total <= HIGHEST)
         bad = jnp.maximum(bad, jnp.where(good, 0.0, 1.0))
 
     @pl.when(jnp.max(bad) > 0.0)
     def exact():
-        one = jnp.ones((16, lanes), BF16)
-
         def step(t, carry):
             qq = jnp.concatenate([qkv[b, t, :HEAD_DIM, :] for b in range(blocks)], axis=1)
 
@@ -151,16 +154,18 @@
                     return jnp.maximum(top, jnp.max(scores(chunk, i), axis=0, keepdims=True))
 
                 top = lax.fori_loop(0, blocks, largest, top)
-            acc = jnp.zeros((32, nq), F32)
+            sums = (jnp.zeros((HEAD_DIM, nq), F32), jnp.zeros((1, nq), F32))
             for chunk in (qkv, *chunks):
 
-                def block(i, acc):
-                    p = jnp.exp(scores(chunk, i) - top).astype(BF16)
-                    v = jnp.concatenate([chunk[i, t, -HEAD_DIM:], one], axis=0)
-                    return acc + jnp.dot(v, p, preferred_element_type=F32)
-
-                acc = lax.fori_loop(0, blocks, block, acc)
-            store(t, acc[:HEAD_DIM] / acc[HEAD_DIM : HEAD_DIM + 1])
+                def block(i, sums):
+                    out, total = sums
+                    p = jnp.exp(scores(chunk, i) - top)
+                    total = total + jnp.sum(p, axis=0, keepdims=True)
+                    v = chunk[i, t, -HEAD_DIM:]
+                    return out + jnp.dot(v, p.astype(BF16), preferred_element_type=F32), total
+
+                sums = lax.fori_loop(0, blocks, block, sums)
+            store(t, sums[0] / sums[1])
             return carry
 
         lax.fori_loop(0, steps, step, 0)
@@ -177,7 +182,7 @@
         out_specs=jax.tree.map(lambda _: VMEM, out_shape),
         scratch_shapes=[
             pltpu.VMEM((steps, keys, 64), BF16),
-            pltpu.VMEM((steps, keys // 256, 32, 256), BF16),
+            pltpu.VMEM((steps, keys // 256, HEAD_DIM, 256), BF16),
         ],
         input_output_aliases=aliases,
         cost_estimate=pl.CostEstimate(
@@ -207,7 +212,7 @@
     steps, sens, width = series.shape
     blocks = lax.axis_size(TM)
     mirror = (lax.axis_index("y1") * 4 + lax.axis_index("x1") * 2).astype(jnp.int32).reshape(1)
-    earlier = lax.ppermute(series, TM, [(i, i + 1) for i in range(blocks - 1)])
+    earlier = lax.ppermute(series[steps - 2 :], TM, [(i, i + 1) for i in range(blocks - 1)])
     conv_own, gain = pl.pallas_call(
         early_kernel,
         out_shape=(
@@ -241,22 +246,24 @@
     from_z = swap(kv, along_z)
     from_y = swap(kv, along_y)
     from_x = swap(kv, along_x)
-    from_xy = swap(kv, along_x | along_y)
-    later = [swap(from_z, m) for m in (along_y, along_x, along_x | along_y)]
+    from_yx = swap(from_y, along_x)
+    from_zy = swap(from_z, along_y)
+    from_zx = swap(from_z, along_x)
+    from_zyx = swap(from_zy, along_x)
     near = qkv.shape[0]
     nq = near * sens
     state = (
         jax.ShapeDtypeStruct((steps, 64, nq), BF16),
-        jax.ShapeDtypeStruct((steps, 32, nq), F32),
+        jax.ShapeDtypeStruct((steps, ROWS, nq), F32),
     )
     qa, acc = attention(begin_kernel, (qkv,), state, 1)
-    acc = attention(more_kernel, (qa, acc, from_z, from_y), state[1], 2, {1: 0})
-    acc = attention(more_kernel, (qa, acc, from_x, from_xy), state[1], 2, {1: 0})
+    for blocks in ((from_y,), (from_z, from_x), (from_yx, from_zy)):
+        acc = attention(more_kernel, (qa, acc, *blocks), state[1], len(blocks), {1: 0})
     attended = attention(
-        functools.partial(end_kernel, 3),
-        (qa, acc, qkv, from_z, from_y, from_x, from_xy, *later),
+        functools.partial(end_kernel, 2),
+        (qa, acc, qkv, from_y, from_z, from_x, from_yx, from_zy, from_zx, from_zyx),
         jax.ShapeDtypeStruct((near, steps, HEAD_DIM, sens), BF16),
-        3,
+        2,
     )
     attended = lax.all_to_all(attended, NEAR, 0, 0, tiled=True)
     return pl.pallas_call(

time: 195 us -> 196 us (level)
  blocking collectives: 19.2 us -> 22.4 us
  starting transfers between devices: 17.1 us -> 14.3 us
    ppermute x7, starting transfers between devices: 15.2 us -> 12.3 us  [swap(): return lax.ppermute(block, SENSOR, [(i, i ^ mask) for i in range(64)])]
    pallas_call x4 -> x5, Pallas kernels: 148 us -> 149 us  [attention(): pl.pallas_call(kernel, out_shape=out_shape, in_specs=[VMEM] * len(operand...]
where the time goes in v4:
time: 196 us
  Pallas kernels  151 us (77%)
  blocking collectives  22.4 us (11%)
  starting transfers between devices  14.3 us (7%)
  waiting for transfers between devices  5.73 us (3%)
  local copies, waits for them, and re-layouts  2.51 us (1%)
    pallas_call x5, Pallas kernels, attention(): pl.pallas_call(kernel, out_shape=out_shape, in_specs=[VMEM] * len(operand...  149 us
    ppermute x7, starting transfers between devices, swap(): return lax.ppermute(block, SENSOR, [(i, i ^ mask) for i in range(64)])  12.3 us
    all_to_all x1, blocking collectives, local(): qkv = lax.all_to_all(qkv, NEAR, 0, 0, tiled=True)  12.3 us
    all_to_all x1, blocking collectives, local(): attended = lax.all_to_all(attended, NEAR, 0, 0, tiled=True)  10.1 us
    ppermute x1, waiting for transfers between devices, local(): lax.ppermute(series[steps - 2:], TM, [(i, i + 1) for i in range(blocks -...  5.71 us
  transfers between devices with their start and end apart: 8, of which 1 were waited for; matrix products, arithmetic and copies ran while one was open for 0% of the time, Pallas kernels for 8%

profile of v4, /device:TPU:192, one launch (start us, length us, event | category | flops | bytes accessed | tf_op | source)
XLA Modules:
  0.0 195.8 jit_solution(16231932130898342375)
XLA Ops:
  0.0 0.9 slice.6
  0.9 1.9 collective-permute-start
  2.8 0.0 copy-start.5
  2.9 0.0 copy-done.1
  2.9 0.6 copy-done.5
  3.5 0.9 copy-done
  4.4 0.2 shard_map.64
  4.7 5.7 %collective-permute-done.earlier = bf16[2,128,128]{2,1,0:T(8,128)(2,1)S(1)} collective-permute-done((bf16[2,128,128]{2,1,0:T(8,128)(2,1)S(1)}, bf16[2,128,128]{2,1,0:T(8,128)(2,1)S(1)}, u32[]{:S(2)}, u32[]{:S(2)}) %collective-permute-start) | collective-permute-done | bytes 65568 | tf_op jit(solution)/shard_map/ppermute | solution.py:215
  10.4 0.0 copy-done.2
  10.4 0.5 shard_map.65
  10.9 12.3 %all_to_all.10.qkv = bf16[8,3,48,128]{3,2,1,0:T(8,128)(2,1)S(1)} all-to-all(bf16[8,3,48,128]{3,2,1,0:T(8,128)(2,1)S(1)} %get-tuple-element.12), channel_id=1, replica_groups=mesh['y1'=2,'y0'=2,'x1'=2,'x0'=2,'z1'=2,'z0'=2,'zh'=2,'core'=2] {'y0','x..., dimensions={0} | all-to-all | bytes 589824 | tf_op jit(solution)/shard_map/all_to_all | solution.py:239
  23.2 1.1 collective-permute-start.1
  24.3 3.4 %collective-permute-start.2 = (bf16[8,3,32,128]{3,2,1,0:T(8,128)(2,1)S(1)}, bf16[8,3,32,128]{3,2,1,0:T(8,128)(2,1)S(1)}, u32[]{:S(2)}, u32[]{:S(2)}) collective-permute-start(bf16[8,3,32,128]{3,2,1,0:T(8,128)(2,1)S(1)} %slice.8), channel_id=1, source_target_pairs={{0,8},{4,12},{8,0},{12,4},{16,24},{20,28},{24,16},{28,20},{32,40},... | collective-permute-start | bytes 589832 | tf_op jit(solution)/shard_map/ppermute | solution.py:243
  27.6 1.7 collective-permute-start.3
  29.4 3.3 %shard_map.66 = (bf16[3,64,1024]{2,1,0:T(8,128)(2,1)S(1)}, f32[3,24,1024]{2,1,0:T(8,128)S(1)}) custom-call(bf16[8,3,48,128]{3,2,1,0:T(8,128)(2,1)S(1)} %all_to_all.10.qkv), custom_call_target="tpu_custom_call" | custom-call | flops 3221225472 | tf_op jit(solution)/shard_map/pallas_call | solution.py:178
  32.7 0.0 collective-permute-done.2.refs_0_.refs_1_
  32.7 0.5 collective-permute-start.5
  33.2 2.2 %collective-permute-start.6 = (bf16[8,3,32,128]{3,2,1,0:T(8,128)(2,1)S(1)}, bf16[8,3,32,128]{3,2,1,0:T(8,128)(2,1)S(1)}, u32[]{:S(2)}, u32[]{:S(2)}) collective-permute-start(bf16[8,3,32,128]{3,2,1,0:T(8,128)(2,1)S(1)} %collective-permute-done.2.refs_0_.refs_1_), channel_id=1, source_target_pairs={{0,48},{4,52},{8,56},{12,60},{16,32},{20,36},{24,40},{28,44},{32,1... | collective-permute-start | bytes 589832 | tf_op jit(solution)/shard_map/ppermute | solution.py:243
  35.4 0.0 collective-permute-done.1.refs_0_
  35.4 1.0 collective-permute-start.4
  36.4 2.7 %shard_map.67.acc_in = f32[3,24,1024]{2,1,0:T(8,128)S(1)} custom-call(bf16[3,64,1024]{2,1,0:T(8,128)(2,1)S(1)} %get-tuple-element.13.qa, f32[3,24,1024]{2,1,0:T(8,128)S(1)} %get-tuple-element.14.acc_in, bf16[8,3,32,128]{3,2,1,0:T(8,128)(2,1)S(1)} %collective-permute-done.1.refs_0_), custom_call_target="tpu_custom_call", output_to_operand_aliasing={{}: (1, {})} | custom-call | flops 3221225472 | tf_op jit(solution)/shard_map/pallas_call | solution.py:178
  39.1 0.0 collective-permute-done.3.refs_1_.refs_2_
  39.1 5.1 %shard_map.68.acc_in = f32[3,24,1024]{2,1,0:T(8,128)S(1)} custom-call(bf16[3,64,1024]{2,1,0:T(8,128)(2,1)S(1)} %get-tuple-element.13.qa, f32[3,24,1024]{2,1,0:T(8,128)S(1)} %shard_map.67.acc_in, bf16[8,3,32,128]{3,2,1,0:T(8,128)(2,1)S(1)} %collective-permute-done.2.refs_0_.refs_1_, ...), custom_call_target="tpu_custom_call", output_to_operand_aliasing={{}: (1, {})} | custom-call | flops 6442450944 | tf_op jit(solution)/shard_map/pallas_call | solution.py:178
  44.2 0.0 collective-permute-done.5.refs_1_.refs_4_
  44.2 2.5 %collective-permute-start.7 = (bf16[8,3,32,128]{3,2,1,0:T(8,128)(2,1)S(1)}, bf16[8,3,32,128]{3,2,1,0:T(8,128)(2,1)S(1)}, u32[]{:S(2)}, u32[]{:S(2)}) collective-permute-start(bf16[8,3,32,128]{3,2,1,0:T(8,128)(2,1)S(1)} %collective-permute-done.5.refs_1_.refs_4_), channel_id=1, source_target_pairs={{0,48},{4,52},{8,56},{12,60},{16,32},{20,36},{24,40},{28,44},{32,1... | collective-permute-start | bytes 589832 | tf_op jit(solution)/shard_map/ppermute | solution.py:243
  46.7 0.0 collective-permute-done.4.refs_0_.refs_3_
  46.7 5.1 %shard_map.69.acc_in = f32[3,24,1024]{2,1,0:T(8,128)S(1)} custom-call(bf16[3,64,1024]{2,1,0:T(8,128)(2,1)S(1)} %get-tuple-element.13.qa, f32[3,24,1024]{2,1,0:T(8,128)S(1)} %shard_map.68.acc_in, bf16[8,3,32,128]{3,2,1,0:T(8,128)(2,1)S(1)} %collective-permute-done.4.refs_0_.refs_3_, ...), custom_call_target="tpu_custom_call", output_to_operand_aliasing={{}: (1, {})} | custom-call | flops 6442450944 | tf_op jit(solution)/shard_map/pallas_call | solution.py:178
  51.7 0.0 collective-permute-done.6.refs_5_
  51.8 0.0 collective-permute-done.7.refs_6_
  51.8 132.8 %shard_map.70 = bf16[8,3,16,128]{3,2,1,0:T(8,128)(2,1)S(1)} custom-call(bf16[3,64,1024]{2,1,0:T(8,128)(2,1)S(1)} %get-tuple-element.13.qa, f32[3,24,1024]{2,1,0:T(8,128)S(1)} %shard_map.69.acc_in, bf16[8,3,48,128]{3,2,1,0:T(8,128)(2,1)S(1)} %all_to_all.10.qkv, bf16[8,3,32,128]{3,2,1,0:T(8,128)(2,1)S(1)} %collective-permute-done.1.refs_0_, ...), custom_call_target="tpu_custom_call" | custom-call | flops 6442450944 | tf_op jit(solution)/shard_map/pallas_call | solution.py:178
  184.6 10.1 %all_to_all.11.attended = bf16[8,3,16,128]{3,2,1,0:T(8,128)(2,1)S(1)} all-to-all(bf16[8,3,16,128]{3,2,1,0:T(8,128)(2,1)S(1)} %shard_map.70), channel_id=1, replica_groups=mesh['y1'=2,'y0'=2,'x1'=2,'x0'=2,'z1'=2,'z0'=2,'zh'=2,'core'=2] {'y0','x..., dimensions={0} | all-to-all | bytes 196608 | tf_op jit(solution)/shard_map/all_to_all | solution.py:268
  194.7 1.1 shard_map.71
  (8 shorter events, 0.0 us)
Async XLA Ops:
  0.0 2.9 %copy-start.1 = (bf16[3,128,128]{2,1,0:T(8,128)(2,1)S(1)}, bf16[3,128,128]{2,1,0:T(8,128)(2,1)}, u32[]{:S(2)}) copy-start(bf16[3,128,128]{2,1,0:T(8,128)(2,1)} %series.3) | copy-start | bytes 294916
  0.9 9.5 %collective-permute-start = (bf16[2,128,128]{2,1,0:T(8,128)(2,1)S(1)}, bf16[2,128,128]{2,1,0:T(8,128)(2,1)S(1)}, u32[]{:S(2)}, u32[]{:S(2)}) collective-permute-start(bf16[2,128,128]{2,1,0:T(8,128)(2,1)S(1)} %slice.6), channel_id=1, source_target_pairs={{0,1},{1,2},{2,3},{4,5},{5,6},{6,7},{8,9},{9,10},{10,11},{12,13},{... | collective-permute-start | bytes 196616 | tf_op jit(solution)/shard_map/ppermute | solution.py:215
  2.8 0.7 copy-start.5
  3.5 0.9 copy-start
  4.4 6.0 %copy-start.2 = (bf16[2,128,128]{2,1,0:T(8,128)(2,1)S(1)}, bf16[2,128,128]{2,1,0:T(8,128)(2,1)}, u32[]{:S(2)}) copy-start(bf16[2,128,128]{2,1,0:T(8,128)(2,1)} %qk_w.1) | copy-start | bytes 196612
  4.4 6.0 %copy-start.3 = (bf16[128,128]{1,0:T(8,128)(2,1)S(1)}, bf16[128,128]{1,0:T(8,128)(2,1)}, u32[]{:S(2)}) copy-start(bf16[128,128]{1,0:T(8,128)(2,1)} %value_w.1) | copy-start | bytes 98308
  23.2 12.2 %collective-permute-start.1 = (bf16[8,3,32,128]{3,2,1,0:T(8,128)(2,1)S(1)}, bf16[8,3,32,128]{3,2,1,0:T(8,128)(2,1)S(1)}, u32[]{:S(2)}, u32[]{:S(2)}) collective-permute-start(bf16[8,3,32,128]{3,2,1,0:T(8,128)(2,1)S(1)} %slice.8), channel_id=1, source_target_pairs={{0,192},{4,196},{8,200},{12,204},{16,208},{20,212},{24,216},{28,22... | collective-permute-start | bytes 589832 | tf_op jit(solution)/shard_map/ppermute | solution.py:243
  24.3 8.4 %collective-permute-start.2 = (bf16[8,3,32,128]{3,2,1,0:T(8,128)(2,1)S(1)}, bf16[8,3,32,128]{3,2,1,0:T(8,128)(2,1)S(1)}, u32[]{:S(2)}, u32[]{:S(2)}) collective-permute-start(bf16[8,3,32,128]{3,2,1,0:T(8,128)(2,1)S(1)} %slice.8), channel_id=1, source_target_pairs={{0,8},{4,12},{8,0},{12,4},{16,24},{20,28},{24,16},{28,20},{32,40},... | collective-permute-start | bytes 589832 | tf_op jit(solution)/shard_map/ppermute | solution.py:243
  27.6 11.5 %collective-permute-start.3 = (bf16[8,3,32,128]{3,2,1,0:T(8,128)(2,1)S(1)}, bf16[8,3,32,128]{3,2,1,0:T(8,128)(2,1)S(1)}, u32[]{:S(2)}, u32[]{:S(2)}) collective-permute-start(bf16[8,3,32,128]{3,2,1,0:T(8,128)(2,1)S(1)} %slice.8), channel_id=1, source_target_pairs={{0,48},{4,52},{8,56},{12,60},{16,32},{20,36},{24,40},{28,44},{32,1... | collective-permute-start | bytes 589832 | tf_op jit(solution)/shard_map/ppermute | solution.py:243
  32.7 11.5 %collective-permute-start.5 = (bf16[8,3,32,128]{3,2,1,0:T(8,128)(2,1)S(1)}, bf16[8,3,32,128]{3,2,1,0:T(8,128)(2,1)S(1)}, u32[]{:S(2)}, u32[]{:S(2)}) collective-permute-start(bf16[8,3,32,128]{3,2,1,0:T(8,128)(2,1)S(1)} %collective-permute-done.2.refs_0_.refs_1_), channel_id=1, source_target_pairs={{0,192},{4,196},{8,200},{12,204},{16,208},{20,212},{24,216},{28,22... | collective-permute-start | bytes 589832 | tf_op jit(solution)/shard_map/ppermute | solution.py:243
  33.2 18.6 %collective-permute-start.6 = (bf16[8,3,32,128]{3,2,1,0:T(8,128)(2,1)S(1)}, bf16[8,3,32,128]{3,2,1,0:T(8,128)(2,1)S(1)}, u32[]{:S(2)}, u32[]{:S(2)}) collective-permute-start(bf16[8,3,32,128]{3,2,1,0:T(8,128)(2,1)S(1)} %collective-permute-done.2.refs_0_.refs_1_), channel_id=1, source_target_pairs={{0,48},{4,52},{8,56},{12,60},{16,32},{20,36},{24,40},{28,44},{32,1... | collective-permute-start | bytes 589832 | tf_op jit(solution)/shard_map/ppermute | solution.py:243
  35.4 11.2 %collective-permute-start.4 = (bf16[8,3,32,128]{3,2,1,0:T(8,128)(2,1)S(1)}, bf16[8,3,32,128]{3,2,1,0:T(8,128)(2,1)S(1)}, u32[]{:S(2)}, u32[]{:S(2)}) collective-permute-start(bf16[8,3,32,128]{3,2,1,0:T(8,128)(2,1)S(1)} %collective-permute-done.1.refs_0_), channel_id=1, source_target_pairs={{0,48},{4,52},{8,56},{12,60},{16,32},{20,36},{24,40},{28,44},{32,1... | collective-permute-start | bytes 589832 | tf_op jit(solution)/shard_map/ppermute | solution.py:243
  44.2 7.5 %collective-permute-start.7 = (bf16[8,3,32,128]{3,2,1,0:T(8,128)(2,1)S(1)}, bf16[8,3,32,128]{3,2,1,0:T(8,128)(2,1)S(1)}, u32[]{:S(2)}, u32[]{:S(2)}) collective-permute-start(bf16[8,3,32,128]{3,2,1,0:T(8,128)(2,1)S(1)} %collective-permute-done.5.refs_1_.refs_4_), channel_id=1, source_target_pairs={{0,48},{4,52},{8,56},{12,60},{16,32},{20,36},{24,40},{28,44},{32,1... | collective-permute-start | bytes 589832 | tf_op jit(solution)/shard_map/ppermute | solution.py:243
  184.6 10.1 %copy-start.4 = (bf16[128,128]{1,0:T(8,128)(2,1)S(1)}, bf16[128,128]{1,0:T(8,128)(2,1)}, u32[]{:S(2)}) copy-start(bf16[128,128]{1,0:T(8,128)(2,1)} %out_w.1) | copy-start | bytes 98308

commit v5 on v4

--- a/solution.py
+++ b/solution.py
@@ -246,9 +246,9 @@
     from_z = swap(kv, along_z)
     from_y = swap(kv, along_y)
     from_x = swap(kv, along_x)
-    from_yx = swap(from_y, along_x)
     from_zy = swap(from_z, along_y)
     from_zx = swap(from_z, along_x)
+    from_xy = swap(from_x, along_y)
     from_zyx = swap(from_zy, along_x)
     near = qkv.shape[0]
     nq = near * sens
@@ -257,13 +257,13 @@
         jax.ShapeDtypeStruct((steps, ROWS, nq), F32),
     )
     qa, acc = attention(begin_kernel, (qkv,), state, 1)
-    for blocks in ((from_y,), (from_z, from_x), (from_yx, from_zy)):
+    for blocks in ((from_z, from_y), (from_x, from_xy)):
         acc = attention(more_kernel, (qa, acc, *blocks), state[1], len(blocks), {1: 0})
     attended = attention(
-        functools.partial(end_kernel, 2),
-        (qa, acc, qkv, from_y, from_z, from_x, from_yx, from_zy, from_zx, from_zyx),
+        functools.partial(end_kernel, 3),
+        (qa, acc, qkv, from_z, from_y, from_x, from_xy, from_zy, from_zx, from_zyx),
         jax.ShapeDtypeStruct((near, steps, HEAD_DIM, sens), BF16),
-        2,
+        3,
     )
     attended = lax.all_to_all(attended, NEAR, 0, 0, tiled=True)
     return pl.pallas_call(

time: 196 us -> 195 us (level)
  blocking collectives: 22.4 us -> 19.7 us
    pallas_call x5 -> x4, Pallas kernels: 149 us -> 149 us  [attention(): pl.pallas_call(kernel, out_shape=out_shape, in_specs=[VMEM] * len(operand...]
  transfers between devices with their start and end apart: 8 -> 8, of which waited for: 1 -> 1; matrix products, arithmetic and copies ran while one was open for 0% -> 0% of each run, Pallas kernels for 8% -> 7%
where the time goes in v5:
time: 195 us
  Pallas kernels  151 us (77%)
  blocking collectives  19.7 us (10%)
  starting transfers between devices  15.9 us (8%)
  waiting for transfers between devices  5.73 us (3%)
  local copies, waits for them, and re-layouts  2.51 us (1%)
    pallas_call x4, Pallas kernels, attention(): pl.pallas_call(kernel, out_shape=out_shape, in_specs=[VMEM] * len(operand...  149 us
    ppermute x7, starting transfers between devices, swap(): return lax.ppermute(block, SENSOR, [(i, i ^ mask) for i in range(64)])  14 us
    all_to_all x1, blocking collectives, local(): qkv = lax.all_to_all(qkv, NEAR, 0, 0, tiled=True)  11.2 us
    all_to_all x1, blocking collectives, local(): attended = lax.all_to_all(attended, NEAR, 0, 0, tiled=True)  8.48 us
    ppermute x1, waiting for transfers between devices, local(): lax.ppermute(series[steps - 2:], TM, [(i, i + 1) for i in range(blocks -...  5.71 us
  transfers between devices with their start and end apart: 8, of which 1 were waited for; matrix products, arithmetic and copies ran while one was open for 0% of the time, Pallas kernels for 7%

profile of v5, /device:TPU:192, one launch (start us, length us, event | category | flops | bytes accessed | tf_op | source)
XLA Modules:
  0.0 194.7 jit_solution(13585568126274302497)
XLA Ops:
  0.0 0.9 slice.6
  0.9 1.9 collective-permute-start
  2.8 0.0 copy-start.5
  2.9 0.0 copy-done.1
  2.9 0.6 copy-done.5
  3.5 0.9 copy-done
  4.4 0.2 shard_map.64
  4.7 5.7 %collective-permute-done.earlier = bf16[2,128,128]{2,1,0:T(8,128)(2,1)S(1)} collective-permute-done((bf16[2,128,128]{2,1,0:T(8,128)(2,1)S(1)}, bf16[2,128,128]{2,1,0:T(8,128)(2,1)S(1)}, u32[]{:S(2)}, u32[]{:S(2)}) %collective-permute-start) | collective-permute-done | bytes 65568 | tf_op jit(solution)/shard_map/ppermute | solution.py:215
  10.4 0.0 copy-done.3
  10.4 0.5 shard_map.65
  10.9 11.2 %all_to_all.10.qkv = bf16[8,3,48,128]{3,2,1,0:T(8,128)(2,1)S(1)} all-to-all(bf16[8,3,48,128]{3,2,1,0:T(8,128)(2,1)S(1)} %get-tuple-element.12), channel_id=1, replica_groups=mesh['y1'=2,'y0'=2,'x1'=2,'x0'=2,'z1'=2,'z0'=2,'zh'=2,'core'=2] {'y0','x..., dimensions={0} | all-to-all | bytes 589824 | tf_op jit(solution)/shard_map/all_to_all | solution.py:239
  22.1 3.5 %collective-permute-start.1 = (bf16[8,3,32,128]{3,2,1,0:T(8,128)(2,1)S(1)}, bf16[8,3,32,128]{3,2,1,0:T(8,128)(2,1)S(1)}, u32[]{:S(2)}, u32[]{:S(2)}) collective-permute-start(bf16[8,3,32,128]{3,2,1,0:T(8,128)(2,1)S(1)} %slice.8), channel_id=1, source_target_pairs={{0,8},{4,12},{8,0},{12,4},{16,24},{20,28},{24,16},{28,20},{32,40},... | collective-permute-start | bytes 589832 | tf_op jit(solution)/shard_map/ppermute | solution.py:243
  25.7 2.0 %collective-permute-start.2 = (bf16[8,3,32,128]{3,2,1,0:T(8,128)(2,1)S(1)}, bf16[8,3,32,128]{3,2,1,0:T(8,128)(2,1)S(1)}, u32[]{:S(2)}, u32[]{:S(2)}) collective-permute-start(bf16[8,3,32,128]{3,2,1,0:T(8,128)(2,1)S(1)} %slice.8), channel_id=1, source_target_pairs={{0,192},{4,196},{8,200},{12,204},{16,208},{20,212},{24,216},{28,22... | collective-permute-start | bytes 589832 | tf_op jit(solution)/shard_map/ppermute | solution.py:243
  27.6 1.9 collective-permute-start.3
  29.5 3.3 %shard_map.66 = (bf16[3,64,1024]{2,1,0:T(8,128)(2,1)S(1)}, f32[3,24,1024]{2,1,0:T(8,128)S(1)}) custom-call(bf16[8,3,48,128]{3,2,1,0:T(8,128)(2,1)S(1)} %all_to_all.10.qkv), custom_call_target="tpu_custom_call" | custom-call | flops 3221225472 | tf_op jit(solution)/shard_map/pallas_call | solution.py:178
  32.8 0.0 collective-permute-done.1.refs_0_
  32.8 1.2 collective-permute-start.5
  34.1 1.4 collective-permute-start.6
  35.5 0.0 collective-permute-done.3.refs_0_.refs_2_
  35.5 2.0 %collective-permute-start.4 = (bf16[8,3,32,128]{3,2,1,0:T(8,128)(2,1)S(1)}, bf16[8,3,32,128]{3,2,1,0:T(8,128)(2,1)S(1)}, u32[]{:S(2)}, u32[]{:S(2)}) collective-permute-start(bf16[8,3,32,128]{3,2,1,0:T(8,128)(2,1)S(1)} %collective-permute-done.3.refs_0_.refs_2_), channel_id=1, source_target_pairs={{0,192},{4,196},{8,200},{12,204},{16,208},{20,212},{24,216},{28,22... | collective-permute-start | bytes 589832 | tf_op jit(solution)/shard_map/ppermute | solution.py:243
  37.5 0.0 collective-permute-done.2.refs_1_
  37.5 5.1 %shard_map.67.acc_in = f32[3,24,1024]{2,1,0:T(8,128)S(1)} custom-call(bf16[3,64,1024]{2,1,0:T(8,128)(2,1)S(1)} %get-tuple-element.13.qa, f32[3,24,1024]{2,1,0:T(8,128)S(1)} %get-tuple-element.14.acc_in, bf16[8,3,32,128]{3,2,1,0:T(8,128)(2,1)S(1)} %collective-permute-done.1.refs_0_, ...), custom_call_target="tpu_custom_call", output_to_operand_aliasing={{}: (1, {})} | custom-call | flops 6442450944 | tf_op jit(solution)/shard_map/pallas_call | solution.py:178
  42.5 0.0 collective-permute-done.5.refs_4_
  42.5 2.0 %collective-permute-start.7 = (bf16[8,3,32,128]{3,2,1,0:T(8,128)(2,1)S(1)}, bf16[8,3,32,128]{3,2,1,0:T(8,128)(2,1)S(1)}, u32[]{:S(2)}, u32[]{:S(2)}) collective-permute-start(bf16[8,3,32,128]{3,2,1,0:T(8,128)(2,1)S(1)} %collective-permute-done.5.refs_4_), channel_id=1, source_target_pairs={{0,48},{4,52},{8,56},{12,60},{16,32},{20,36},{24,40},{28,44},{32,1... | collective-permute-start | bytes 589832 | tf_op jit(solution)/shard_map/ppermute | solution.py:243
  44.6 0.0 collective-permute-done.4.refs_1_.refs_3_
  44.6 5.1 %shard_map.68.acc_in = f32[3,24,1024]{2,1,0:T(8,128)S(1)} custom-call(bf16[3,64,1024]{2,1,0:T(8,128)(2,1)S(1)} %get-tuple-element.13.qa, f32[3,24,1024]{2,1,0:T(8,128)S(1)} %shard_map.67.acc_in, bf16[8,3,32,128]{3,2,1,0:T(8,128)(2,1)S(1)} %collective-permute-done.3.refs_0_.refs_2_, ...), custom_call_target="tpu_custom_call", output_to_operand_aliasing={{}: (1, {})} | custom-call | flops 6442450944 | tf_op jit(solution)/shard_map/pallas_call | solution.py:178
  49.7 0.0 collective-permute-done.6.refs_5_
  49.7 0.0 collective-permute-done.7.refs_6_
  49.7 135.4 %shard_map.69 = bf16[8,3,16,128]{3,2,1,0:T(8,128)(2,1)S(1)} custom-call(bf16[3,64,1024]{2,1,0:T(8,128)(2,1)S(1)} %get-tuple-element.13.qa, f32[3,24,1024]{2,1,0:T(8,128)S(1)} %shard_map.68.acc_in, bf16[8,3,48,128]{3,2,1,0:T(8,128)(2,1)S(1)} %all_to_all.10.qkv, bf16[8,3,32,128]{3,2,1,0:T(8,128)(2,1)S(1)} %collective-permute-done.1.refs_0_, ...), custom_call_target="tpu_custom_call" | custom-call | flops 9663676416 | tf_op jit(solution)/shard_map/pallas_call | solution.py:178
  185.1 8.5 %all_to_all.11.attended = bf16[8,3,16,128]{3,2,1,0:T(8,128)(2,1)S(1)} all-to-all(bf16[8,3,16,128]{3,2,1,0:T(8,128)(2,1)S(1)} %shard_map.69), channel_id=1, replica_groups=mesh['y1'=2,'y0'=2,'x1'=2,'x0'=2,'z1'=2,'z0'=2,'zh'=2,'core'=2] {'y0','x..., dimensions={0} | all-to-all | bytes 196608 | tf_op jit(solution)/shard_map/all_to_all | solution.py:268
  193.6 0.0 copy-done.4
  193.6 1.1 shard_map.70
  (7 shorter events, 0.0 us)
Async XLA Ops:
  0.0 2.9 %copy-start.1 = (bf16[3,128,128]{2,1,0:T(8,128)(2,1)S(1)}, bf16[3,128,128]{2,1,0:T(8,128)(2,1)}, u32[]{:S(2)}) copy-start(bf16[3,128,128]{2,1,0:T(8,128)(2,1)} %series.3) | copy-start | bytes 294916
  0.9 9.5 %collective-permute-start = (bf16[2,128,128]{2,1,0:T(8,128)(2,1)S(1)}, bf16[2,128,128]{2,1,0:T(8,128)(2,1)S(1)}, u32[]{:S(2)}, u32[]{:S(2)}) collective-permute-start(bf16[2,128,128]{2,1,0:T(8,128)(2,1)S(1)} %slice.6), channel_id=1, source_target_pairs={{0,1},{1,2},{2,3},{4,5},{5,6},{6,7},{8,9},{9,10},{10,11},{12,13},{... | collective-permute-start | bytes 196616 | tf_op jit(solution)/shard_map/ppermute | solution.py:215
  2.8 0.7 copy-start.5
  3.5 0.9 copy-start
  4.4 6.0 %copy-start.2 = (bf16[2,128,128]{2,1,0:T(8,128)(2,1)S(1)}, bf16[2,128,128]{2,1,0:T(8,128)(2,1)}, u32[]{:S(2)}) copy-start(bf16[2,128,128]{2,1,0:T(8,128)(2,1)} %qk_w.1) | copy-start | bytes 196612
  4.4 6.0 %copy-start.3 = (bf16[128,128]{1,0:T(8,128)(2,1)S(1)}, bf16[128,128]{1,0:T(8,128)(2,1)}, u32[]{:S(2)}) copy-start(bf16[128,128]{1,0:T(8,128)(2,1)} %value_w.1) | copy-start | bytes 98308
  22.1 10.7 %collective-permute-start.1 = (bf16[8,3,32,128]{3,2,1,0:T(8,128)(2,1)S(1)}, bf16[8,3,32,128]{3,2,1,0:T(8,128)(2,1)S(1)}, u32[]{:S(2)}, u32[]{:S(2)}) collective-permute-start(bf16[8,3,32,128]{3,2,1,0:T(8,128)(2,1)S(1)} %slice.8), channel_id=1, source_target_pairs={{0,8},{4,12},{8,0},{12,4},{16,24},{20,28},{24,16},{28,20},{32,40},... | collective-permute-start | bytes 589832 | tf_op jit(solution)/shard_map/ppermute | solution.py:243
  25.7 11.8 %collective-permute-start.2 = (bf16[8,3,32,128]{3,2,1,0:T(8,128)(2,1)S(1)}, bf16[8,3,32,128]{3,2,1,0:T(8,128)(2,1)S(1)}, u32[]{:S(2)}, u32[]{:S(2)}) collective-permute-start(bf16[8,3,32,128]{3,2,1,0:T(8,128)(2,1)S(1)} %slice.8), channel_id=1, source_target_pairs={{0,192},{4,196},{8,200},{12,204},{16,208},{20,212},{24,216},{28,22... | collective-permute-start | bytes 589832 | tf_op jit(solution)/shard_map/ppermute | solution.py:243
  27.6 7.9 %collective-permute-start.3 = (bf16[8,3,32,128]{3,2,1,0:T(8,128)(2,1)S(1)}, bf16[8,3,32,128]{3,2,1,0:T(8,128)(2,1)S(1)}, u32[]{:S(2)}, u32[]{:S(2)}) collective-permute-start(bf16[8,3,32,128]{3,2,1,0:T(8,128)(2,1)S(1)} %slice.8), channel_id=1, source_target_pairs={{0,48},{4,52},{8,56},{12,60},{16,32},{20,36},{24,40},{28,44},{32,1... | collective-permute-start | bytes 589832 | tf_op jit(solution)/shard_map/ppermute | solution.py:243
  32.8 9.7 %collective-permute-start.5 = (bf16[8,3,32,128]{3,2,1,0:T(8,128)(2,1)S(1)}, bf16[8,3,32,128]{3,2,1,0:T(8,128)(2,1)S(1)}, u32[]{:S(2)}, u32[]{:S(2)}) collective-permute-start(bf16[8,3,32,128]{3,2,1,0:T(8,128)(2,1)S(1)} %collective-permute-done.1.refs_0_), channel_id=1, source_target_pairs={{0,192},{4,196},{8,200},{12,204},{16,208},{20,212},{24,216},{28,22... | collective-permute-start | bytes 589832 | tf_op jit(solution)/shard_map/ppermute | solution.py:243
  34.1 15.6 %collective-permute-start.6 = (bf16[8,3,32,128]{3,2,1,0:T(8,128)(2,1)S(1)}, bf16[8,3,32,128]{3,2,1,0:T(8,128)(2,1)S(1)}, u32[]{:S(2)}, u32[]{:S(2)}) collective-permute-start(bf16[8,3,32,128]{3,2,1,0:T(8,128)(2,1)S(1)} %collective-permute-done.1.refs_0_), channel_id=1, source_target_pairs={{0,48},{4,52},{8,56},{12,60},{16,32},{20,36},{24,40},{28,44},{32,1... | collective-permute-start | bytes 589832 | tf_op jit(solution)/shard_map/ppermute | solution.py:243
  35.5 9.1 %collective-permute-start.4 = (bf16[8,3,32,128]{3,2,1,0:T(8,128)(2,1)S(1)}, bf16[8,3,32,128]{3,2,1,0:T(8,128)(2,1)S(1)}, u32[]{:S(2)}, u32[]{:S(2)}) collective-permute-start(bf16[8,3,32,128]{3,2,1,0:T(8,128)(2,1)S(1)} %collective-permute-done.3.refs_0_.refs_2_), channel_id=1, source_target_pairs={{0,192},{4,196},{8,200},{12,204},{16,208},{20,212},{24,216},{28,22... | collective-permute-start | bytes 589832 | tf_op jit(solution)/shard_map/ppermute | solution.py:243
  42.5 7.1 %collective-permute-start.7 = (bf16[8,3,32,128]{3,2,1,0:T(8,128)(2,1)S(1)}, bf16[8,3,32,128]{3,2,1,0:T(8,128)(2,1)S(1)}, u32[]{:S(2)}, u32[]{:S(2)}) collective-permute-start(bf16[8,3,32,128]{3,2,1,0:T(8,128)(2,1)S(1)} %collective-permute-done.5.refs_4_), channel_id=1, source_target_pairs={{0,48},{4,52},{8,56},{12,60},{16,32},{20,36},{24,40},{28,44},{32,1... | collective-permute-start | bytes 589832 | tf_op jit(solution)/shard_map/ppermute | solution.py:243
  185.1 8.5 %copy-start.4 = (bf16[128,128]{1,0:T(8,128)(2,1)S(1)}, bf16[128,128]{1,0:T(8,128)(2,1)}, u32[]{:S(2)}) copy-start(bf16[128,128]{1,0:T(8,128)(2,1)} %out_w.1) | copy-start | bytes 98308

commit v6 on v5

--- a/solution.py
+++ b/solution.py
@@ -15,7 +15,7 @@
 AXES = ("y1", "y0", "x1", "x0", "z1", "z0", "zh", "core")
 SENSOR = AXES[:6]
 TM = AXES[6:]
-NEAR = ("y0", "x0", "z0")
+NEAR = ("z0", "y0", "x0")
 VMEM = pl.BlockSpec(memory_space=pltpu.VMEM)
 SMEM = pl.BlockSpec(memory_space=pltpu.SMEM)
 TILE = 512
@@ -66,16 +66,16 @@
 
 
 def absorb(t, qq, acc, chunks, ka, va):
-    blocks, lanes = chunks[0].shape[0], chunks[0].shape[3]
+    lanes = chunks[0].shape[3]
     one = jnp.ones((16, 2 * lanes), BF16)
-    for c, chunk in enumerate(chunks):
-        for p in range(blocks // 2):
+    pairs = 0
+    for chunk in chunks:
+        for p in range(chunk.shape[0] // 2):
             kv = jnp.concatenate([chunk[2 * p, t, -32:], chunk[2 * p + 1, t, -32:]], axis=1)
             k = kv[:HEAD_DIM]
-            pair = c * (blocks // 2) + p
-            ka[pair * 256 : (pair + 1) * 256, :] = jnp.concatenate([k, k, k, one], axis=0).T
-            va[pair] = kv[HEAD_DIM:]
-    pairs = len(chunks) * (blocks // 2)
+            ka[pairs * 256 : (pairs + 1) * 256, :] = jnp.concatenate([k, k, k, one], axis=0).T
+            va[pairs] = kv[HEAD_DIM:]
+            pairs += 1
     parts = []
     for start in range(0, acc.shape[1], TILE):
         cut = slice(start, start + TILE)
@@ -153,7 +153,7 @@
                 def largest(i, top):
                     return jnp.maximum(top, jnp.max(scores(chunk, i), axis=0, keepdims=True))
 
-                top = lax.fori_loop(0, blocks, largest, top)
+                top = lax.fori_loop(0, chunk.shape[0], largest, top)
             sums = (jnp.zeros((HEAD_DIM, nq), F32), jnp.zeros((1, nq), F32))
             for chunk in (qkv, *chunks):
 
@@ -164,15 +164,14 @@
                     v = chunk[i, t, -HEAD_DIM:]
                     return out + jnp.dot(v, p.astype(BF16), preferred_element_type=F32), total
 
-                sums = lax.fori_loop(0, blocks, block, sums)
+                sums = lax.fori_loop(0, chunk.shape[0], block, sums)
             store(t, sums[0] / sums[1])
             return carry
 
         lax.fori_loop(0, steps, step, 0)
 
 
-def attention(kernel, operands, out_shape, chunks, aliases={}):
-    shape = operands[-1].shape
+def attention(kernel, operands, out_shape, chunks, shape, aliases={}):
     near, steps, _, sens = shape
     keys = chunks * near * sens
     return pl.pallas_call(
@@ -211,7 +210,7 @@
 def local(series, conv_weight, qk_weight, value_weight, out_weight, norm_gain):
     steps, sens, width = series.shape
     blocks = lax.axis_size(TM)
-    mirror = (lax.axis_index("y1") * 4 + lax.axis_index("x1") * 2).astype(jnp.int32).reshape(1)
+    mirror = (lax.axis_index("y1") * 2 + lax.axis_index("x1") * 1).astype(jnp.int32).reshape(1)
     earlier = lax.ppermute(series[steps - 2 :], TM, [(i, i + 1) for i in range(blocks - 1)])
     conv_own, gain = pl.pallas_call(
         early_kernel,
@@ -247,8 +246,7 @@
     from_y = swap(kv, along_y)
     from_x = swap(kv, along_x)
     from_zy = swap(from_z, along_y)
-    from_zx = swap(from_z, along_x)
-    from_xy = swap(from_x, along_y)
+    beyond_x = swap(jnp.concatenate([from_z, from_y], axis=0), along_x)
     from_zyx = swap(from_zy, along_x)
     near = qkv.shape[0]
     nq = near * sens
@@ -256,14 +254,16 @@
         jax.ShapeDtypeStruct((steps, 64, nq), BF16),
         jax.ShapeDtypeStruct((steps, ROWS, nq), F32),
     )
-    qa, acc = attention(begin_kernel, (qkv,), state, 1)
-    for blocks in ((from_z, from_y), (from_x, from_xy)):
-        acc = attention(more_kernel, (qa, acc, *blocks), state[1], len(blocks), {1: 0})
+    shape = kv.shape
+    qa, acc = attention(begin_kernel, (qkv,), state, 1, shape)
+    for pair in ((from_z, from_y), (from_x, from_zy)):
+        acc = attention(more_kernel, (qa, acc, *pair), state[1], 2, shape, {1: 0})
     attended = attention(
-        functools.partial(end_kernel, 3),
-        (qa, acc, qkv, from_z, from_y, from_x, from_xy, from_zy, from_zx, from_zyx),
+        functools.partial(end_kernel, 2),
+        (qa, acc, qkv, from_z, from_y, from_x, from_zy, beyond_x, from_zyx),
         jax.ShapeDtypeStruct((near, steps, HEAD_DIM, sens), BF16),
         3,
+        shape,
     )
     attended = lax.all_to_all(attended, NEAR, 0, 0, tiled=True)
     return pl.pallas_call(

time: 195 us -> 194 us (level)
    ppermute x7 -> x6, starting transfers between devices: 14 us -> 12.6 us  [swap(): return lax.ppermute(block, SENSOR, [(i, i ^ mask) for i in range(64)])]
  transfers between devices with their start and end apart: 8 -> 7, of which waited for: 1 -> 2; matrix products, arithmetic and copies ran while one was open for 0% -> 0% of each run, Pallas kernels for 7% -> 7%
where the time goes in v6:
time: 194 us; the launch traced here: 193 us
  Pallas kernels  151 us (78%)
  blocking collectives  19.5 us (10%)
  starting transfers between devices  14.5 us (7%)
  waiting for transfers between devices  6.19 us (3%)
  local copies, waits for them, and re-layouts  2.51 us (1%)
    pallas_call x4, Pallas kernels, attention(): pl.pallas_call(kernel, out_shape=out_shape, in_specs=[VMEM] * len(operand...  149 us
    ppermute x6, starting transfers between devices, swap(): return lax.ppermute(block, SENSOR, [(i, i ^ mask) for i in range(64)])  12.6 us
    all_to_all x1, blocking collectives, local(): qkv = lax.all_to_all(qkv, NEAR, 0, 0, tiled=True)  11.1 us
    all_to_all x1, blocking collectives, local(): attended = lax.all_to_all(attended, NEAR, 0, 0, tiled=True)  8.35 us
    ppermute x1, waiting for transfers between devices, local(): lax.ppermute(series[steps - 2:], TM, [(i, i + 1) for i in range(blocks -...  5.71 us
  transfers between devices with their start and end apart: 7, of which 2 were waited for; matrix products, arithmetic and copies ran while one was open for 0% of the time, Pallas kernels for 7%

profile of v6, /device:TPU:192, one launch (start us, length us, event | category | flops | bytes accessed | tf_op | source)
XLA Modules:
  0.0 193.4 jit_solution(1793455559944303954)
XLA Ops:
  0.0 0.0 copy-start.1
  0.0 0.9 slice.6
  0.9 1.9 collective-permute-start
  2.8 0.0 copy-start.5
  2.9 0.0 copy-done.1
  2.9 0.6 copy-done.5
  3.5 0.9 copy-done
  4.4 0.2 shard_map.64
  4.7 5.7 %collective-permute-done.earlier = bf16[2,128,128]{2,1,0:T(8,128)(2,1)S(1)} collective-permute-done((bf16[2,128,128]{2,1,0:T(8,128)(2,1)S(1)}, bf16[2,128,128]{2,1,0:T(8,128)(2,1)S(1)}, u32[]{:S(2)}, u32[]{:S(2)}) %collective-permute-start) | collective-permute-done | bytes 65568 | tf_op jit(solution)/shard_map/ppermute | solution.py:214
  10.4 0.0 copy-done.2
  10.4 0.0 copy-done.3
  10.4 0.5 shard_map.65
  10.9 11.1 %all_to_all.10.qkv = bf16[8,3,48,128]{3,2,1,0:T(8,128)(2,1)S(1)} all-to-all(bf16[8,3,48,128]{3,2,1,0:T(8,128)(2,1)S(1)} %get-tuple-element.12), channel_id=1, replica_groups=mesh['y1'=2,'y0'=2,'x1'=2,'x0'=2,'z1'=2,'z0'=2,'zh'=2,'core'=2] {'z0','y..., dimensions={0} | all-to-all | bytes 589824 | tf_op jit(solution)/shard_map/all_to_all | solution.py:238
  22.1 3.5 %collective-permute-start.1 = (bf16[8,3,32,128]{3,2,1,0:T(8,128)(2,1)S(1)}, bf16[8,3,32,128]{3,2,1,0:T(8,128)(2,1)S(1)}, u32[]{:S(2)}, u32[]{:S(2)}) collective-permute-start(bf16[8,3,32,128]{3,2,1,0:T(8,128)(2,1)S(1)} %slice.8), channel_id=1, source_target_pairs={{0,8},{4,12},{8,0},{12,4},{16,24},{20,28},{24,16},{28,20},{32,40},... | collective-permute-start | bytes 589832 | tf_op jit(solution)/shard_map/ppermute | solution.py:242
  25.6 1.9 collective-permute-start.2
  27.5 2.0 %collective-permute-start.3 = (bf16[8,3,32,128]{3,2,1,0:T(8,128)(2,1)S(1)}, bf16[8,3,32,128]{3,2,1,0:T(8,128)(2,1)S(1)}, u32[]{:S(2)}, u32[]{:S(2)}) collective-permute-start(bf16[8,3,32,128]{3,2,1,0:T(8,128)(2,1)S(1)} %slice.8), channel_id=1, source_target_pairs={{0,48},{4,52},{8,56},{12,60},{16,32},{20,36},{24,40},{28,44},{32,1... | collective-permute-start | bytes 589832 | tf_op jit(solution)/shard_map/ppermute | solution.py:242
  29.5 3.3 %shard_map.66 = (bf16[3,64,1024]{2,1,0:T(8,128)(2,1)S(1)}, f32[3,24,1024]{2,1,0:T(8,128)S(1)}) custom-call(bf16[8,3,48,128]{3,2,1,0:T(8,128)(2,1)S(1)} %all_to_all.10.qkv), custom_call_target="tpu_custom_call" | custom-call | flops 3221225472 | tf_op jit(solution)/shard_map/pallas_call | solution.py:177
  32.8 0.0 collective-permute-done.1.refs_0_
  32.9 0.0 collective-permute-done.2.refs_1_
  32.9 1.5 collective-permute-start.5
  34.4 2.1 %collective-permute-start.4 = (bf16[8,3,32,128]{3,2,1,0:T(8,128)(2,1)S(1)}, bf16[8,3,32,128]{3,2,1,0:T(8,128)(2,1)S(1)}, u32[]{:S(2)}, u32[]{:S(2)}) collective-permute-start(bf16[8,3,32,128]{3,2,1,0:T(8,128)(2,1)S(1)} %collective-permute-done.1.refs_0_), channel_id=1, source_target_pairs={{0,192},{4,196},{8,200},{12,204},{16,208},{20,212},{24,216},{28,22... | collective-permute-start | bytes 589832 | tf_op jit(solution)/shard_map/ppermute | solution.py:242
  36.5 5.1 %shard_map.67.acc_in = f32[3,24,1024]{2,1,0:T(8,128)S(1)} custom-call(bf16[3,64,1024]{2,1,0:T(8,128)(2,1)S(1)} %get-tuple-element.13.qa, f32[3,24,1024]{2,1,0:T(8,128)S(1)} %get-tuple-element.14.acc_in, bf16[8,3,32,128]{3,2,1,0:T(8,128)(2,1)S(1)} %collective-permute-done.1.refs_0_, ...), custom_call_target="tpu_custom_call", output_to_operand_aliasing={{}: (1, {})} | custom-call | flops 6442450944 | tf_op jit(solution)/shard_map/pallas_call | solution.py:177
  41.6 0.0 collective-permute-done.4.refs_1_.refs_3_
  41.6 1.5 collective-permute-start.6
  43.1 0.0 collective-permute-done.3.refs_0_.refs_2_
  43.1 5.1 %shard_map.68.acc_in = f32[3,24,1024]{2,1,0:T(8,128)S(1)} custom-call(bf16[3,64,1024]{2,1,0:T(8,128)(2,1)S(1)} %get-tuple-element.13.qa, f32[3,24,1024]{2,1,0:T(8,128)S(1)} %shard_map.67.acc_in, bf16[8,3,32,128]{3,2,1,0:T(8,128)(2,1)S(1)} %collective-permute-done.3.refs_0_.refs_2_, ...), custom_call_target="tpu_custom_call", output_to_operand_aliasing={{}: (1, {})} | custom-call | flops 6442450944 | tf_op jit(solution)/shard_map/pallas_call | solution.py:177
  48.2 0.0 collective-permute-done.5.refs_4_
  48.2 0.5 collective-permute-done.6.refs_5_
  48.6 135.3 %shard_map.69 = bf16[8,3,16,128]{3,2,1,0:T(8,128)(2,1)S(1)} custom-call(bf16[3,64,1024]{2,1,0:T(8,128)(2,1)S(1)} %get-tuple-element.13.qa, f32[3,24,1024]{2,1,0:T(8,128)S(1)} %shard_map.68.acc_in, bf16[8,3,48,128]{3,2,1,0:T(8,128)(2,1)S(1)} %all_to_all.10.qkv, bf16[8,3,32,128]{3,2,1,0:T(8,128)(2,1)S(1)} %collective-permute-done.1.refs_0_, ...), custom_call_target="tpu_custom_call" | custom-call | flops 9663676416 | tf_op jit(solution)/shard_map/pallas_call | solution.py:177
  184.0 8.3 %all_to_all.11.attended = bf16[8,3,16,128]{3,2,1,0:T(8,128)(2,1)S(1)} all-to-all(bf16[8,3,16,128]{3,2,1,0:T(8,128)(2,1)S(1)} %shard_map.69), channel_id=1, replica_groups=mesh['y1'=2,'y0'=2,'x1'=2,'x0'=2,'z1'=2,'z0'=2,'zh'=2,'core'=2] {'z0','y..., dimensions={0} | all-to-all | bytes 196608 | tf_op jit(solution)/shard_map/all_to_all | solution.py:268
  192.3 0.0 copy-done.4
  192.3 1.1 shard_map.70
  (6 shorter events, 0.1 us)
Async XLA Ops:
  0.0 2.9 %copy-start.1 = (bf16[3,128,128]{2,1,0:T(8,128)(2,1)S(1)}, bf16[3,128,128]{2,1,0:T(8,128)(2,1)}, u32[]{:S(2)}) copy-start(bf16[3,128,128]{2,1,0:T(8,128)(2,1)} %series.3) | copy-start | bytes 294916
  0.9 9.5 %collective-permute-start = (bf16[2,128,128]{2,1,0:T(8,128)(2,1)S(1)}, bf16[2,128,128]{2,1,0:T(8,128)(2,1)S(1)}, u32[]{:S(2)}, u32[]{:S(2)}) collective-permute-start(bf16[2,128,128]{2,1,0:T(8,128)(2,1)S(1)} %slice.6), channel_id=1, source_target_pairs={{0,1},{1,2},{2,3},{4,5},{5,6},{6,7},{8,9},{9,10},{10,11},{12,13},{... | collective-permute-start | bytes 196616 | tf_op jit(solution)/shard_map/ppermute | solution.py:214
  2.8 0.7 copy-start.5
  3.5 0.9 copy-start
  4.4 6.0 %copy-start.2 = (bf16[2,128,128]{2,1,0:T(8,128)(2,1)S(1)}, bf16[2,128,128]{2,1,0:T(8,128)(2,1)}, u32[]{:S(2)}) copy-start(bf16[2,128,128]{2,1,0:T(8,128)(2,1)} %qk_w.1) | copy-start | bytes 196612
  4.4 6.0 %copy-start.3 = (bf16[128,128]{1,0:T(8,128)(2,1)S(1)}, bf16[128,128]{1,0:T(8,128)(2,1)}, u32[]{:S(2)}) copy-start(bf16[128,128]{1,0:T(8,128)(2,1)} %value_w.1) | copy-start | bytes 98308
  22.1 10.8 %collective-permute-start.1 = (bf16[8,3,32,128]{3,2,1,0:T(8,128)(2,1)S(1)}, bf16[8,3,32,128]{3,2,1,0:T(8,128)(2,1)S(1)}, u32[]{:S(2)}, u32[]{:S(2)}) collective-permute-start(bf16[8,3,32,128]{3,2,1,0:T(8,128)(2,1)S(1)} %slice.8), channel_id=1, source_target_pairs={{0,8},{4,12},{8,0},{12,4},{16,24},{20,28},{24,16},{28,20},{32,40},... | collective-permute-start | bytes 589832 | tf_op jit(solution)/shard_map/ppermute | solution.py:242
  25.6 7.2 %collective-permute-start.2 = (bf16[8,3,32,128]{3,2,1,0:T(8,128)(2,1)S(1)}, bf16[8,3,32,128]{3,2,1,0:T(8,128)(2,1)S(1)}, u32[]{:S(2)}, u32[]{:S(2)}) collective-permute-start(bf16[8,3,32,128]{3,2,1,0:T(8,128)(2,1)S(1)} %slice.8), channel_id=1, source_target_pairs={{0,192},{4,196},{8,200},{12,204},{16,208},{20,212},{24,216},{28,22... | collective-permute-start | bytes 589832 | tf_op jit(solution)/shard_map/ppermute | solution.py:242
  27.5 15.6 %collective-permute-start.3 = (bf16[8,3,32,128]{3,2,1,0:T(8,128)(2,1)S(1)}, bf16[8,3,32,128]{3,2,1,0:T(8,128)(2,1)S(1)}, u32[]{:S(2)}, u32[]{:S(2)}) collective-permute-start(bf16[8,3,32,128]{3,2,1,0:T(8,128)(2,1)S(1)} %slice.8), channel_id=1, source_target_pairs={{0,48},{4,52},{8,56},{12,60},{16,32},{20,36},{24,40},{28,44},{32,1... | collective-permute-start | bytes 589832 | tf_op jit(solution)/shard_map/ppermute | solution.py:242
  32.9 15.3 %collective-permute-start.5 = (bf16[16,3,32,128]{3,2,1,0:T(8,128)(2,1)S(1)}, bf16[16,3,32,128]{3,2,1,0:T(8,128)(2,1)S(1)}, u32[]{:S(2)}, u32[]{:S(2)}) collective-permute-start(bf16[16,3,32,128]{3,2,1,0:T(8,128)(2,1)S(1)} %pad_maximum_fusion), channel_id=1, source_target_pairs={{0,48},{4,52},{8,56},{12,60},{16,32},{20,36},{24,40},{28,44},{32,1... | collective-permute-start | bytes 1179656 | tf_op jit(solution)/shard_map/ppermute | solution.py:242
  34.4 7.2 %collective-permute-start.4 = (bf16[8,3,32,128]{3,2,1,0:T(8,128)(2,1)S(1)}, bf16[8,3,32,128]{3,2,1,0:T(8,128)(2,1)S(1)}, u32[]{:S(2)}, u32[]{:S(2)}) collective-permute-start(bf16[8,3,32,128]{3,2,1,0:T(8,128)(2,1)S(1)} %collective-permute-done.1.refs_0_), channel_id=1, source_target_pairs={{0,192},{4,196},{8,200},{12,204},{16,208},{20,212},{24,216},{28,22... | collective-permute-start | bytes 589832 | tf_op jit(solution)/shard_map/ppermute | solution.py:242
  41.6 7.1 %collective-permute-start.6 = (bf16[8,3,32,128]{3,2,1,0:T(8,128)(2,1)S(1)}, bf16[8,3,32,128]{3,2,1,0:T(8,128)(2,1)S(1)}, u32[]{:S(2)}, u32[]{:S(2)}) collective-permute-start(bf16[8,3,32,128]{3,2,1,0:T(8,128)(2,1)S(1)} %collective-permute-done.4.refs_1_.refs_3_), channel_id=1, source_target_pairs={{0,48},{4,52},{8,56},{12,60},{16,32},{20,36},{24,40},{28,44},{32,1... | collective-permute-start | bytes 589832 | tf_op jit(solution)/shard_map/ppermute | solution.py:242
  183.9 8.4 %copy-start.4 = (bf16[128,128]{1,0:T(8,128)(2,1)S(1)}, bf16[128,128]{1,0:T(8,128)(2,1)}, u32[]{:S(2)}) copy-start(bf16[128,128]{1,0:T(8,128)(2,1)} %out_w.1) | copy-start | bytes 98308

commit v7 on v6

--- a/solution.py
+++ b/solution.py
@@ -32,37 +32,50 @@
     return high, mid, low
 
 
-def early_kernel(series, conv_w, gain, conv_ref, gain_ref):
+def project(conv, own, qk_w, value_w, flip, steps, hidden_ref, qkv_ref):
+    sens = qkv_ref.shape[-1]
+    width = own.shape[1]
+    gate = jax.nn.sigmoid(conv[:, width:])
+    hidden = (own.astype(F32) + conv[:, :width] * gate).astype(BF16)
+    hidden_ref[steps[0] * sens : (steps[-1] + 1) * sens, :] = hidden
+    for part, weight in enumerate((qk_w[0], qk_w[1], value_w[...])):
+        rows = jnp.dot(hidden, weight, preferred_element_type=F32).astype(BF16)
+        for i, t in enumerate(steps):
+            cols = rows[i * sens : (i + 1) * sens].T
+            for h in range(HEADS):
+                qkv_ref[h ^ flip, t, part * HEAD_DIM : (part + 1) * HEAD_DIM, :] = cols[
+                    h * HEAD_DIM : (h + 1) * HEAD_DIM
+                ]
+
+
+def early_kernel(
+    mirror, series, conv_w, qk_w, value_w, gain, conv_ref, gain_ref, hidden_ref, qkv_ref
+):
     steps, sens, width = series.shape
     own = series[...].reshape(steps * sens, width)
-    conv_ref[...] = jnp.dot(own, conv_w[0], preferred_element_type=F32)
+    conv = jnp.dot(own, conv_w[0], preferred_element_type=F32)
     for tap in (1, 2):
         rows = (steps - tap) * sens
-        conv_ref[tap * sens :, :] += jnp.dot(own[:rows], conv_w[tap], preferred_element_type=F32)
+        late = jnp.dot(own[:rows], conv_w[tap], preferred_element_type=F32)
+        conv = jnp.concatenate([conv[: tap * sens], conv[tap * sens :] + late], axis=0)
     gain_ref[...] = gain[...]
-
-
-def first_kernel(mirror, earlier, series, conv_own, conv_w, qk_w, value_w, hidden_ref, qkv_ref):
-    flip = mirror[0]
+    conv_ref[...] = conv[: 2 * sens]
+    free = list(range(2, steps))
+    project(
+        conv[2 * sens :], own[2 * sens :], qk_w, value_w, mirror[0], free, hidden_ref, qkv_ref
+    )
+
+
+def first_kernel(
+    mirror, earlier, series, conv_own, conv_w, qk_w, value_w, hidden_in, qkv_in, hidden_ref, qkv_ref
+):
     steps, sens, width = series.shape
-    own = series[...].reshape(steps * sens, width)
+    own = series[:2].reshape(2 * sens, width)
     before = earlier[...].reshape(2 * sens, width)
     late = jnp.dot(before, conv_w[2], preferred_element_type=F32)
     near = jnp.dot(before[sens:], conv_w[1], preferred_element_type=F32)
     late = late + jnp.concatenate([near, jnp.zeros_like(near)], axis=0)
-    conv = conv_own[...]
-    conv = jnp.concatenate([conv[: 2 * sens] + late, conv[2 * sens :]], axis=0)
-    gate = jax.nn.sigmoid(conv[:, width:])
-    hidden = (own.astype(F32) + conv[:, :width] * gate).astype(BF16)
-    hidden_ref[...] = hidden
-    for part, weight in enumerate((qk_w[0], qk_w[1], value_w[...])):
-        rows = jnp.dot(hidden, weight, preferred_element_type=F32).astype(BF16)
-        for t in range(steps):
-            cols = rows[t * sens : (t + 1) * sens].T
-            for h in range(HEADS):
-                qkv_ref[h ^ flip, t, part * HEAD_DIM : (part + 1) * HEAD_DIM, :] = cols[
-                    h * HEAD_DIM : (h + 1) * HEAD_DIM
-                ]
+    project(conv_own[...] + late, own, qk_w, value_w, mirror[0], [0, 1], hidden_ref, qkv_ref)
 
 
 def absorb(t, qq, acc, chunks, ka, va):
@@ -101,7 +114,7 @@
         for b in range(blocks):
             parts = split3(qkv[b, t, :HEAD_DIM, :].astype(F32) * (0.25 * LOG2E))
             qa[:48, b * lanes : (b + 1) * lanes] = jnp.concatenate(parts, axis=0)
-        k = jnp.concatenate([qkv[0, t, HEAD_DIM:32, :], qkv[1, t, HEAD_DIM:32, :]], axis=1)
+        k = qkv[0, t, HEAD_DIM:32, :]
         k = jnp.concatenate([k, k, k], axis=0).T
         sample = jnp.dot(k, qa[:48, :], preferred_element_type=F32)
         shift = split3(-jnp.max(sample, axis=0, keepdims=True))
@@ -212,29 +225,32 @@
     blocks = lax.axis_size(TM)
     mirror = (lax.axis_index("y1") * 2 + lax.axis_index("x1") * 1).astype(jnp.int32).reshape(1)
     earlier = lax.ppermute(series[steps - 2 :], TM, [(i, i + 1) for i in range(blocks - 1)])
-    conv_own, gain = pl.pallas_call(
+    made = (
+        jax.ShapeDtypeStruct((steps * sens, width), BF16),
+        jax.ShapeDtypeStruct((HEADS, steps, 3 * HEAD_DIM, sens), BF16),
+    )
+    conv_own, gain, hidden, qkv = pl.pallas_call(
         early_kernel,
         out_shape=(
-            jax.ShapeDtypeStruct((steps * sens, 2 * width), F32),
+            jax.ShapeDtypeStruct((2 * sens, 2 * width), F32),
             jax.ShapeDtypeStruct((1, width), F32),
+            *made,
         ),
-        in_specs=[VMEM] * 3,
-        out_specs=(VMEM, VMEM),
+        in_specs=[SMEM] + [VMEM] * 5,
+        out_specs=(VMEM,) * 4,
         cost_estimate=pl.CostEstimate(
             flops=2 * 3 * steps * sens * width * 2 * width, bytes_accessed=0, transcendentals=0
         ),
         compiler_params=pltpu.CompilerParams(vmem_limit_bytes=32 << 20),
-    )(series, conv_weight, norm_gain.reshape(1, width))
+    )(mirror, series, conv_weight, qk_weight, value_weight, norm_gain.reshape(1, width))
     hidden, qkv = pl.pallas_call(
         first_kernel,
-        out_shape=(
-            jax.ShapeDtypeStruct((steps * sens, width), BF16),
-            jax.ShapeDtypeStruct((HEADS, steps, 3 * HEAD_DIM, sens), BF16),
-        ),
-        in_specs=[SMEM] + [VMEM] * 6,
+        out_shape=made,
+        in_specs=[SMEM] + [VMEM] * 8,
         out_specs=(VMEM, VMEM),
+        input_output_aliases={7: 0, 8: 1},
         compiler_params=pltpu.CompilerParams(vmem_limit_bytes=32 << 20),
-    )(mirror, earlier, series, conv_own, conv_weight, qk_weight, value_weight)
+    )(mirror, earlier, series, conv_own, conv_weight, qk_weight, value_weight, hidden, qkv)
     qkv = lax.all_to_all(qkv, NEAR, 0, 0, tiled=True)
     kv = qkv[:, :, HEAD_DIM:, :]
 

time: 194 us -> 194 us (level)
  no operation moved by 1% of the time
where the time goes in v7:
time: 194 us; the launch traced here: 193 us
  Pallas kernels  151 us (78%)
  blocking collectives  19.5 us (10%)
  starting transfers between devices  14.5 us (7%)
  waiting for transfers between devices  5.16 us (3%)
  local copies, waits for them, and re-layouts  3.33 us (2%)
    pallas_call x4, Pallas kernels, attention(): pl.pallas_call(kernel, out_shape=out_shape, in_specs=[VMEM] * len(operand...  149 us
    ppermute x6, starting transfers between devices, swap(): return lax.ppermute(block, SENSOR, [(i, i ^ mask) for i in range(64)])  12.6 us
    all_to_all x1, blocking collectives, local(): qkv = lax.all_to_all(qkv, NEAR, 0, 0, tiled=True)  11.1 us
    all_to_all x1, blocking collectives, local(): attended = lax.all_to_all(attended, NEAR, 0, 0, tiled=True)  8.35 us
    ppermute x1, waiting for transfers between devices, local(): lax.ppermute(series[steps - 2:], TM, [(i, i + 1) for i in range(blocks -...  4.63 us
  transfers between devices with their start and end apart: 7, of which 2 were waited for; matrix products, arithmetic and copies ran while one was open for 0% of the time, Pallas kernels for 7%

profile of v7, /device:TPU:192, one launch (start us, length us, event | category | flops | bytes accessed | tf_op | source)
XLA Modules:
  0.0 193.3 jit_solution(2042115500741572785)
XLA Ops:
  0.0 0.0 copy-start.1
  0.0 0.9 slice.6
  0.9 1.9 collective-permute-start
  2.8 0.0 copy-start.5
  2.9 0.0 copy-done.1
  2.9 0.0 copy-done.3
  2.9 0.6 copy-done.5
  3.5 0.9 copy-done
  4.4 0.8 copy-done.2
  5.3 0.5 shard_map.64
  5.8 4.6 %collective-permute-done.earlier = bf16[2,128,128]{2,1,0:T(8,128)(2,1)S(1)} collective-permute-done((bf16[2,128,128]{2,1,0:T(8,128)(2,1)S(1)}, bf16[2,128,128]{2,1,0:T(8,128)(2,1)S(1)}, u32[]{:S(2)}, u32[]{:S(2)}) %collective-permute-start) | collective-permute-done | bytes 65568 | tf_op jit(solution)/shard_map/ppermute | solution.py:227
  10.4 0.5 shard_map.65
  10.9 11.1 %all_to_all.10.qkv = bf16[8,3,48,128]{3,2,1,0:T(8,128)(2,1)S(1)} all-to-all(bf16[8,3,48,128]{3,2,1,0:T(8,128)(2,1)S(1)} %get-tuple-element.16), channel_id=1, replica_groups=mesh['y1'=2,'y0'=2,'x1'=2,'x0'=2,'z1'=2,'z0'=2,'zh'=2,'core'=2] {'z0','y..., dimensions={0} | all-to-all | bytes 589824 | tf_op jit(solution)/shard_map/all_to_all | solution.py:254
  22.0 3.5 %collective-permute-start.1 = (bf16[8,3,32,128]{3,2,1,0:T(8,128)(2,1)S(1)}, bf16[8,3,32,128]{3,2,1,0:T(8,128)(2,1)S(1)}, u32[]{:S(2)}, u32[]{:S(2)}) collective-permute-start(bf16[8,3,32,128]{3,2,1,0:T(8,128)(2,1)S(1)} %slice.8), channel_id=1, source_target_pairs={{0,8},{4,12},{8,0},{12,4},{16,24},{20,28},{24,16},{28,20},{32,40},... | collective-permute-start | bytes 589832 | tf_op jit(solution)/shard_map/ppermute | solution.py:258
  25.6 1.9 collective-permute-start.2
  27.5 2.0 %collective-permute-start.3 = (bf16[8,3,32,128]{3,2,1,0:T(8,128)(2,1)S(1)}, bf16[8,3,32,128]{3,2,1,0:T(8,128)(2,1)S(1)}, u32[]{:S(2)}, u32[]{:S(2)}) collective-permute-start(bf16[8,3,32,128]{3,2,1,0:T(8,128)(2,1)S(1)} %slice.8), channel_id=1, source_target_pairs={{0,48},{4,52},{8,56},{12,60},{16,32},{20,36},{24,40},{28,44},{32,1... | collective-permute-start | bytes 589832 | tf_op jit(solution)/shard_map/ppermute | solution.py:258
  29.5 3.2 %shard_map.66 = (bf16[3,64,1024]{2,1,0:T(8,128)(2,1)S(1)}, f32[3,24,1024]{2,1,0:T(8,128)S(1)}) custom-call(bf16[8,3,48,128]{3,2,1,0:T(8,128)(2,1)S(1)} %all_to_all.10.qkv), custom_call_target="tpu_custom_call" | custom-call | flops 3221225472 | tf_op jit(solution)/shard_map/pallas_call | solution.py:190
  32.7 0.0 collective-permute-done.1.refs_0_
  32.7 0.0 collective-permute-done.2.refs_1_
  32.8 1.6 collective-permute-start.5
  34.4 2.1 %collective-permute-start.4 = (bf16[8,3,32,128]{3,2,1,0:T(8,128)(2,1)S(1)}, bf16[8,3,32,128]{3,2,1,0:T(8,128)(2,1)S(1)}, u32[]{:S(2)}, u32[]{:S(2)}) collective-permute-start(bf16[8,3,32,128]{3,2,1,0:T(8,128)(2,1)S(1)} %collective-permute-done.1.refs_0_), channel_id=1, source_target_pairs={{0,192},{4,196},{8,200},{12,204},{16,208},{20,212},{24,216},{28,22... | collective-permute-start | bytes 589832 | tf_op jit(solution)/shard_map/ppermute | solution.py:258
  36.5 5.1 %shard_map.67.acc_in = f32[3,24,1024]{2,1,0:T(8,128)S(1)} custom-call(bf16[3,64,1024]{2,1,0:T(8,128)(2,1)S(1)} %get-tuple-element.17.qa, f32[3,24,1024]{2,1,0:T(8,128)S(1)} %get-tuple-element.18.acc_in, bf16[8,3,32,128]{3,2,1,0:T(8,128)(2,1)S(1)} %collective-permute-done.1.refs_0_, ...), custom_call_target="tpu_custom_call", output_to_operand_aliasing={{}: (1, {})} | custom-call | flops 6442450944 | tf_op jit(solution)/shard_map/pallas_call | solution.py:190
  41.5 0.0 collective-permute-done.4.refs_1_.refs_3_
  41.5 1.5 collective-permute-start.6
  43.0 0.0 collective-permute-done.3.refs_0_.refs_2_
  43.0 5.1 %shard_map.68.acc_in = f32[3,24,1024]{2,1,0:T(8,128)S(1)} custom-call(bf16[3,64,1024]{2,1,0:T(8,128)(2,1)S(1)} %get-tuple-element.17.qa, f32[3,24,1024]{2,1,0:T(8,128)S(1)} %shard_map.67.acc_in, bf16[8,3,32,128]{3,2,1,0:T(8,128)(2,1)S(1)} %collective-permute-done.3.refs_0_.refs_2_, ...), custom_call_target="tpu_custom_call", output_to_operand_aliasing={{}: (1, {})} | custom-call | flops 6442450944 | tf_op jit(solution)/shard_map/pallas_call | solution.py:190
  48.1 0.0 collective-permute-done.5.refs_4_
  48.1 0.5 collective-permute-done.6.refs_5_
  48.6 135.3 %shard_map.69 = bf16[8,3,16,128]{3,2,1,0:T(8,128)(2,1)S(1)} custom-call(bf16[3,64,1024]{2,1,0:T(8,128)(2,1)S(1)} %get-tuple-element.17.qa, f32[3,24,1024]{2,1,0:T(8,128)S(1)} %shard_map.68.acc_in, bf16[8,3,48,128]{3,2,1,0:T(8,128)(2,1)S(1)} %all_to_all.10.qkv, bf16[8,3,32,128]{3,2,1,0:T(8,128)(2,1)S(1)} %collective-permute-done.1.refs_0_, ...), custom_call_target="tpu_custom_call" | custom-call | flops 9663676416 | tf_op jit(solution)/shard_map/pallas_call | solution.py:190
  183.9 8.3 %all_to_all.11.attended = bf16[8,3,16,128]{3,2,1,0:T(8,128)(2,1)S(1)} all-to-all(bf16[8,3,16,128]{3,2,1,0:T(8,128)(2,1)S(1)} %shard_map.69), channel_id=1, replica_groups=mesh['y1'=2,'y0'=2,'x1'=2,'x0'=2,'z1'=2,'z0'=2,'zh'=2,'core'=2] {'z0','y..., dimensions={0} | all-to-all | bytes 196608 | tf_op jit(solution)/shard_map/all_to_all | solution.py:284
  192.3 0.0 copy-done.4
  192.3 1.1 shard_map.70
  (6 shorter events, 0.1 us)
Async XLA Ops:
  0.0 2.9 %copy-start.1 = (bf16[3,128,128]{2,1,0:T(8,128)(2,1)S(1)}, bf16[3,128,128]{2,1,0:T(8,128)(2,1)}, u32[]{:S(2)}) copy-start(bf16[3,128,128]{2,1,0:T(8,128)(2,1)} %series.3) | copy-start | bytes 294916
  0.0 2.9 %copy-start.3 = (bf16[128,128]{1,0:T(8,128)(2,1)S(1)}, bf16[128,128]{1,0:T(8,128)(2,1)}, u32[]{:S(2)}) copy-start(bf16[128,128]{1,0:T(8,128)(2,1)} %value_w.3) | copy-start | bytes 98308
  0.9 9.5 %collective-permute-start = (bf16[2,128,128]{2,1,0:T(8,128)(2,1)S(1)}, bf16[2,128,128]{2,1,0:T(8,128)(2,1)S(1)}, u32[]{:S(2)}, u32[]{:S(2)}) collective-permute-start(bf16[2,128,128]{2,1,0:T(8,128)(2,1)S(1)} %slice.6), channel_id=1, source_target_pairs={{0,1},{1,2},{2,3},{4,5},{5,6},{6,7},{8,9},{9,10},{10,11},{12,13},{... | collective-permute-start | bytes 196616 | tf_op jit(solution)/shard_map/ppermute | solution.py:227
  2.8 0.7 copy-start.5
  3.5 0.9 copy-start
  4.4 0.8 copy-start.2
  22.0 10.7 %collective-permute-start.1 = (bf16[8,3,32,128]{3,2,1,0:T(8,128)(2,1)S(1)}, bf16[8,3,32,128]{3,2,1,0:T(8,128)(2,1)S(1)}, u32[]{:S(2)}, u32[]{:S(2)}) collective-permute-start(bf16[8,3,32,128]{3,2,1,0:T(8,128)(2,1)S(1)} %slice.8), channel_id=1, source_target_pairs={{0,8},{4,12},{8,0},{12,4},{16,24},{20,28},{24,16},{28,20},{32,40},... | collective-permute-start | bytes 589832 | tf_op jit(solution)/shard_map/ppermute | solution.py:258
  25.6 7.1 %collective-permute-start.2 = (bf16[8,3,32,128]{3,2,1,0:T(8,128)(2,1)S(1)}, bf16[8,3,32,128]{3,2,1,0:T(8,128)(2,1)S(1)}, u32[]{:S(2)}, u32[]{:S(2)}) collective-permute-start(bf16[8,3,32,128]{3,2,1,0:T(8,128)(2,1)S(1)} %slice.8), channel_id=1, source_target_pairs={{0,192},{4,196},{8,200},{12,204},{16,208},{20,212},{24,216},{28,22... | collective-permute-start | bytes 589832 | tf_op jit(solution)/shard_map/ppermute | solution.py:258
  27.5 15.5 %collective-permute-start.3 = (bf16[8,3,32,128]{3,2,1,0:T(8,128)(2,1)S(1)}, bf16[8,3,32,128]{3,2,1,0:T(8,128)(2,1)S(1)}, u32[]{:S(2)}, u32[]{:S(2)}) collective-permute-start(bf16[8,3,32,128]{3,2,1,0:T(8,128)(2,1)S(1)} %slice.8), channel_id=1, source_target_pairs={{0,48},{4,52},{8,56},{12,60},{16,32},{20,36},{24,40},{28,44},{32,1... | collective-permute-start | bytes 589832 | tf_op jit(solution)/shard_map/ppermute | solution.py:258
  32.8 15.3 %collective-permute-start.5 = (bf16[16,3,32,128]{3,2,1,0:T(8,128)(2,1)S(1)}, bf16[16,3,32,128]{3,2,1,0:T(8,128)(2,1)S(1)}, u32[]{:S(2)}, u32[]{:S(2)}) collective-permute-start(bf16[16,3,32,128]{3,2,1,0:T(8,128)(2,1)S(1)} %pad_maximum_fusion), channel_id=1, source_target_pairs={{0,48},{4,52},{8,56},{12,60},{16,32},{20,36},{24,40},{28,44},{32,1... | collective-permute-start | bytes 1179656 | tf_op jit(solution)/shard_map/ppermute | solution.py:258
  34.4 7.2 %collective-permute-start.4 = (bf16[8,3,32,128]{3,2,1,0:T(8,128)(2,1)S(1)}, bf16[8,3,32,128]{3,2,1,0:T(8,128)(2,1)S(1)}, u32[]{:S(2)}, u32[]{:S(2)}) collective-permute-start(bf16[8,3,32,128]{3,2,1,0:T(8,128)(2,1)S(1)} %collective-permute-done.1.refs_0_), channel_id=1, source_target_pairs={{0,192},{4,196},{8,200},{12,204},{16,208},{20,212},{24,216},{28,22... | collective-permute-start | bytes 589832 | tf_op jit(solution)/shard_map/ppermute | solution.py:258
  41.5 7.1 %collective-permute-start.6 = (bf16[8,3,32,128]{3,2,1,0:T(8,128)(2,1)S(1)}, bf16[8,3,32,128]{3,2,1,0:T(8,128)(2,1)S(1)}, u32[]{:S(2)}, u32[]{:S(2)}) collective-permute-start(bf16[8,3,32,128]{3,2,1,0:T(8,128)(2,1)S(1)} %collective-permute-done.4.refs_1_.refs_3_), channel_id=1, source_target_pairs={{0,48},{4,52},{8,56},{12,60},{16,32},{20,36},{24,40},{28,44},{32,1... | collective-permute-start | bytes 589832 | tf_op jit(solution)/shard_map/ppermute | solution.py:258
  183.9 8.4 %copy-start.4 = (bf16[128,128]{1,0:T(8,128)(2,1)S(1)}, bf16[128,128]{1,0:T(8,128)(2,1)}, u32[]{:S(2)}) copy-start(bf16[128,128]{1,0:T(8,128)(2,1)} %out_w.1) | copy-start | bytes 98308

commit v8 on v7

--- a/solution.py
+++ b/solution.py
@@ -210,14 +210,17 @@
     flip = mirror[0]
     heads, steps, dim, sens = attended.shape
     width = heads * dim
-    for t in range(steps):
-        rows = jnp.concatenate([attended[h ^ flip, t] for h in range(heads)], axis=0).T
-        mixed = jnp.dot(rows, out_w[...], preferred_element_type=F32)
-        mixed = mixed + hidden[t * sens : (t + 1) * sens, :].astype(F32)
-        mean = jnp.mean(mixed, axis=-1, keepdims=True)
-        centred = mixed - mean
-        var = jnp.mean(centred * centred, axis=-1, keepdims=True)
-        out_ref[t] = (centred / jnp.sqrt(var + 1e-5) * gain[...]).astype(BF16)
+    cols = [
+        jnp.concatenate([attended[h ^ flip, t] for h in range(heads)], axis=0)
+        for t in range(steps)
+    ]
+    rows = jnp.concatenate(cols, axis=1).T
+    mixed = jnp.dot(rows, out_w[...], preferred_element_type=F32) + hidden[...].astype(F32)
+    mean = jnp.mean(mixed, axis=-1, keepdims=True)
+    centred = mixed - mean
+    var = jnp.mean(centred * centred, axis=-1, keepdims=True)
+    normed = (centred / jnp.sqrt(var + 1e-5) * gain[...]).astype(BF16)
+    out_ref[...] = normed.reshape(steps, sens, heads * dim)
 
 
 def local(series, conv_weight, qk_weight, value_weight, out_weight, norm_gain):

time: 194 us -> 194 us (level)
  no operation moved by 1% of the time
where the time goes in v8:
time: 194 us; the launch traced here: 193 us
  Pallas kernels  151 us (78%)
  blocking collectives  19.5 us (10%)
  starting transfers between devices  14.5 us (7%)
  waiting for transfers between devices  5.16 us (3%)
  local copies, waits for them, and re-layouts  3.33 us (2%)
    pallas_call x4, Pallas kernels, attention(): pl.pallas_call(kernel, out_shape=out_shape, in_specs=[VMEM] * len(operand...  149 us
    ppermute x6, starting transfers between devices, swap(): return lax.ppermute(block, SENSOR, [(i, i ^ mask) for i in range(64)])  12.6 us
    all_to_all x1, blocking collectives, local(): qkv = lax.all_to_all(qkv, NEAR, 0, 0, tiled=True)  11.1 us
    all_to_all x1, blocking collectives, local(): attended = lax.all_to_all(attended, NEAR, 0, 0, tiled=True)  8.35 us
    ppermute x1, waiting for transfers between devices, local(): lax.ppermute(series[steps - 2:], TM, [(i, i + 1) for i in range(blocks -...  4.63 us
  transfers between devices with their start and end apart: 7, of which 2 were waited for; matrix products, arithmetic and copies ran while one was open for 0% of the time, Pallas kernels for 7%

profile of v8, /device:TPU:192, one launch (start us, length us, event | category | flops | bytes accessed | tf_op | source)
XLA Modules:
  0.0 193.3 jit_solution(3305752183440344032)
XLA Ops:
  0.0 0.0 copy-start.1
  0.0 0.9 slice.6
  0.9 1.9 collective-permute-start
  2.8 0.0 copy-start.5
  2.9 0.0 copy-done.1
  2.9 0.0 copy-done.3
  2.9 0.6 copy-done.5
  3.5 0.9 copy-done
  4.4 0.8 copy-done.2
  5.3 0.5 shard_map.64
  5.8 4.6 %collective-permute-done.earlier = bf16[2,128,128]{2,1,0:T(8,128)(2,1)S(1)} collective-permute-done((bf16[2,128,128]{2,1,0:T(8,128)(2,1)S(1)}, bf16[2,128,128]{2,1,0:T(8,128)(2,1)S(1)}, u32[]{:S(2)}, u32[]{:S(2)}) %collective-permute-start) | collective-permute-done | bytes 65568 | tf_op jit(solution)/shard_map/ppermute | solution.py:230
  10.4 0.5 shard_map.65
  10.9 11.1 %all_to_all.10.qkv = bf16[8,3,48,128]{3,2,1,0:T(8,128)(2,1)S(1)} all-to-all(bf16[8,3,48,128]{3,2,1,0:T(8,128)(2,1)S(1)} %get-tuple-element.16), channel_id=1, replica_groups=mesh['y1'=2,'y0'=2,'x1'=2,'x0'=2,'z1'=2,'z0'=2,'zh'=2,'core'=2] {'z0','y..., dimensions={0} | all-to-all | bytes 589824 | tf_op jit(solution)/shard_map/all_to_all | solution.py:257
  22.0 3.5 %collective-permute-start.1 = (bf16[8,3,32,128]{3,2,1,0:T(8,128)(2,1)S(1)}, bf16[8,3,32,128]{3,2,1,0:T(8,128)(2,1)S(1)}, u32[]{:S(2)}, u32[]{:S(2)}) collective-permute-start(bf16[8,3,32,128]{3,2,1,0:T(8,128)(2,1)S(1)} %slice.8), channel_id=1, source_target_pairs={{0,8},{4,12},{8,0},{12,4},{16,24},{20,28},{24,16},{28,20},{32,40},... | collective-permute-start | bytes 589832 | tf_op jit(solution)/shard_map/ppermute | solution.py:261
  25.6 1.9 collective-permute-start.2
  27.5 2.0 %collective-permute-start.3 = (bf16[8,3,32,128]{3,2,1,0:T(8,128)(2,1)S(1)}, bf16[8,3,32,128]{3,2,1,0:T(8,128)(2,1)S(1)}, u32[]{:S(2)}, u32[]{:S(2)}) collective-permute-start(bf16[8,3,32,128]{3,2,1,0:T(8,128)(2,1)S(1)} %slice.8), channel_id=1, source_target_pairs={{0,48},{4,52},{8,56},{12,60},{16,32},{20,36},{24,40},{28,44},{32,1... | collective-permute-start | bytes 589832 | tf_op jit(solution)/shard_map/ppermute | solution.py:261
  29.5 3.2 %shard_map.66 = (bf16[3,64,1024]{2,1,0:T(8,128)(2,1)S(1)}, f32[3,24,1024]{2,1,0:T(8,128)S(1)}) custom-call(bf16[8,3,48,128]{3,2,1,0:T(8,128)(2,1)S(1)} %all_to_all.10.qkv), custom_call_target="tpu_custom_call" | custom-call | flops 3221225472 | tf_op jit(solution)/shard_map/pallas_call | solution.py:190
  32.7 0.0 collective-permute-done.1.refs_0_
  32.7 0.0 collective-permute-done.2.refs_1_
  32.8 1.6 collective-permute-start.5
  34.4 2.1 %collective-permute-start.4 = (bf16[8,3,32,128]{3,2,1,0:T(8,128)(2,1)S(1)}, bf16[8,3,32,128]{3,2,1,0:T(8,128)(2,1)S(1)}, u32[]{:S(2)}, u32[]{:S(2)}) collective-permute-start(bf16[8,3,32,128]{3,2,1,0:T(8,128)(2,1)S(1)} %collective-permute-done.1.refs_0_), channel_id=1, source_target_pairs={{0,192},{4,196},{8,200},{12,204},{16,208},{20,212},{24,216},{28,22... | collective-permute-start | bytes 589832 | tf_op jit(solution)/shard_map/ppermute | solution.py:261
  36.5 5.1 %shard_map.67.acc_in = f32[3,24,1024]{2,1,0:T(8,128)S(1)} custom-call(bf16[3,64,1024]{2,1,0:T(8,128)(2,1)S(1)} %get-tuple-element.17.qa, f32[3,24,1024]{2,1,0:T(8,128)S(1)} %get-tuple-element.18.acc_in, bf16[8,3,32,128]{3,2,1,0:T(8,128)(2,1)S(1)} %collective-permute-done.1.refs_0_, ...), custom_call_target="tpu_custom_call", output_to_operand_aliasing={{}: (1, {})} | custom-call | flops 6442450944 | tf_op jit(solution)/shard_map/pallas_call | solution.py:190
  41.5 0.0 collective-permute-done.4.refs_1_.refs_3_
  41.5 1.5 collective-permute-start.6
  43.0 0.0 collective-permute-done.3.refs_0_.refs_2_
  43.0 5.1 %shard_map.68.acc_in = f32[3,24,1024]{2,1,0:T(8,128)S(1)} custom-call(bf16[3,64,1024]{2,1,0:T(8,128)(2,1)S(1)} %get-tuple-element.17.qa, f32[3,24,1024]{2,1,0:T(8,128)S(1)} %shard_map.67.acc_in, bf16[8,3,32,128]{3,2,1,0:T(8,128)(2,1)S(1)} %collective-permute-done.3.refs_0_.refs_2_, ...), custom_call_target="tpu_custom_call", output_to_operand_aliasing={{}: (1, {})} | custom-call | flops 6442450944 | tf_op jit(solution)/shard_map/pallas_call | solution.py:190
  48.1 0.0 collective-permute-done.5.refs_4_
  48.1 0.5 collective-permute-done.6.refs_5_
  48.6 135.3 %shard_map.69 = bf16[8,3,16,128]{3,2,1,0:T(8,128)(2,1)S(1)} custom-call(bf16[3,64,1024]{2,1,0:T(8,128)(2,1)S(1)} %get-tuple-element.17.qa, f32[3,24,1024]{2,1,0:T(8,128)S(1)} %shard_map.68.acc_in, bf16[8,3,48,128]{3,2,1,0:T(8,128)(2,1)S(1)} %all_to_all.10.qkv, bf16[8,3,32,128]{3,2,1,0:T(8,128)(2,1)S(1)} %collective-permute-done.1.refs_0_, ...), custom_call_target="tpu_custom_call" | custom-call | flops 9663676416 | tf_op jit(solution)/shard_map/pallas_call | solution.py:190
  183.9 8.3 %all_to_all.11.attended = bf16[8,3,16,128]{3,2,1,0:T(8,128)(2,1)S(1)} all-to-all(bf16[8,3,16,128]{3,2,1,0:T(8,128)(2,1)S(1)} %shard_map.69), channel_id=1, replica_groups=mesh['y1'=2,'y0'=2,'x1'=2,'x0'=2,'z1'=2,'z0'=2,'zh'=2,'core'=2] {'z0','y..., dimensions={0} | all-to-all | bytes 196608 | tf_op jit(solution)/shard_map/all_to_all | solution.py:287
  192.3 0.0 copy-done.4
  192.3 1.1 shard_map.70
  (6 shorter events, 0.1 us)
Async XLA Ops:
  0.0 2.9 %copy-start.1 = (bf16[3,128,128]{2,1,0:T(8,128)(2,1)S(1)}, bf16[3,128,128]{2,1,0:T(8,128)(2,1)}, u32[]{:S(2)}) copy-start(bf16[3,128,128]{2,1,0:T(8,128)(2,1)} %series.3) | copy-start | bytes 294916
  0.0 2.9 %copy-start.3 = (bf16[128,128]{1,0:T(8,128)(2,1)S(1)}, bf16[128,128]{1,0:T(8,128)(2,1)}, u32[]{:S(2)}) copy-start(bf16[128,128]{1,0:T(8,128)(2,1)} %value_w.3) | copy-start | bytes 98308
  0.9 9.5 %collective-permute-start = (bf16[2,128,128]{2,1,0:T(8,128)(2,1)S(1)}, bf16[2,128,128]{2,1,0:T(8,128)(2,1)S(1)}, u32[]{:S(2)}, u32[]{:S(2)}) collective-permute-start(bf16[2,128,128]{2,1,0:T(8,128)(2,1)S(1)} %slice.6), channel_id=1, source_target_pairs={{0,1},{1,2},{2,3},{4,5},{5,6},{6,7},{8,9},{9,10},{10,11},{12,13},{... | collective-permute-start | bytes 196616 | tf_op jit(solution)/shard_map/ppermute | solution.py:230
  2.8 0.7 copy-start.5
  3.5 0.9 copy-start
  4.4 0.8 copy-start.2
  22.0 10.7 %collective-permute-start.1 = (bf16[8,3,32,128]{3,2,1,0:T(8,128)(2,1)S(1)}, bf16[8,3,32,128]{3,2,1,0:T(8,128)(2,1)S(1)}, u32[]{:S(2)}, u32[]{:S(2)}) collective-permute-start(bf16[8,3,32,128]{3,2,1,0:T(8,128)(2,1)S(1)} %slice.8), channel_id=1, source_target_pairs={{0,8},{4,12},{8,0},{12,4},{16,24},{20,28},{24,16},{28,20},{32,40},... | collective-permute-start | bytes 589832 | tf_op jit(solution)/shard_map/ppermute | solution.py:261
  25.6 7.1 %collective-permute-start.2 = (bf16[8,3,32,128]{3,2,1,0:T(8,128)(2,1)S(1)}, bf16[8,3,32,128]{3,2,1,0:T(8,128)(2,1)S(1)}, u32[]{:S(2)}, u32[]{:S(2)}) collective-permute-start(bf16[8,3,32,128]{3,2,1,0:T(8,128)(2,1)S(1)} %slice.8), channel_id=1, source_target_pairs={{0,192},{4,196},{8,200},{12,204},{16,208},{20,212},{24,216},{28,22... | collective-permute-start | bytes 589832 | tf_op jit(solution)/shard_map/ppermute | solution.py:261
  27.5 15.5 %collective-permute-start.3 = (bf16[8,3,32,128]{3,2,1,0:T(8,128)(2,1)S(1)}, bf16[8,3,32,128]{3,2,1,0:T(8,128)(2,1)S(1)}, u32[]{:S(2)}, u32[]{:S(2)}) collective-permute-start(bf16[8,3,32,128]{3,2,1,0:T(8,128)(2,1)S(1)} %slice.8), channel_id=1, source_target_pairs={{0,48},{4,52},{8,56},{12,60},{16,32},{20,36},{24,40},{28,44},{32,1... | collective-permute-start | bytes 589832 | tf_op jit(solution)/shard_map/ppermute | solution.py:261
  32.8 15.3 %collective-permute-start.5 = (bf16[16,3,32,128]{3,2,1,0:T(8,128)(2,1)S(1)}, bf16[16,3,32,128]{3,2,1,0:T(8,128)(2,1)S(1)}, u32[]{:S(2)}, u32[]{:S(2)}) collective-permute-start(bf16[16,3,32,128]{3,2,1,0:T(8,128)(2,1)S(1)} %pad_maximum_fusion), channel_id=1, source_target_pairs={{0,48},{4,52},{8,56},{12,60},{16,32},{20,36},{24,40},{28,44},{32,1... | collective-permute-start | bytes 1179656 | tf_op jit(solution)/shard_map/ppermute | solution.py:261
  34.4 7.2 %collective-permute-start.4 = (bf16[8,3,32,128]{3,2,1,0:T(8,128)(2,1)S(1)}, bf16[8,3,32,128]{3,2,1,0:T(8,128)(2,1)S(1)}, u32[]{:S(2)}, u32[]{:S(2)}) collective-permute-start(bf16[8,3,32,128]{3,2,1,0:T(8,128)(2,1)S(1)} %collective-permute-done.1.refs_0_), channel_id=1, source_target_pairs={{0,192},{4,196},{8,200},{12,204},{16,208},{20,212},{24,216},{28,22... | collective-permute-start | bytes 589832 | tf_op jit(solution)/shard_map/ppermute | solution.py:261
  41.5 7.1 %collective-permute-start.6 = (bf16[8,3,32,128]{3,2,1,0:T(8,128)(2,1)S(1)}, bf16[8,3,32,128]{3,2,1,0:T(8,128)(2,1)S(1)}, u32[]{:S(2)}, u32[]{:S(2)}) collective-permute-start(bf16[8,3,32,128]{3,2,1,0:T(8,128)(2,1)S(1)} %collective-permute-done.4.refs_1_.refs_3_), channel_id=1, source_target_pairs={{0,48},{4,52},{8,56},{12,60},{16,32},{20,36},{24,40},{28,44},{32,1... | collective-permute-start | bytes 589832 | tf_op jit(solution)/shard_map/ppermute | solution.py:261
  183.9 8.4 %copy-start.4 = (bf16[128,128]{1,0:T(8,128)(2,1)S(1)}, bf16[128,128]{1,0:T(8,128)(2,1)}, u32[]{:S(2)}) copy-start(bf16[128,128]{1,0:T(8,128)(2,1)} %out_w.1) | copy-start | bytes 98308
